TPU v7x, 128 devices: a whole 4x4x4 slice. The times are simulated.
128 devices in a mesh: rows: 16 (over y, x), inner: 8 (over z, core).
Axes of the slice: x: 4, y: 4, z: 4, core: 2. Of those that a mesh axis runs over, the one named last changes fastest.
Arguments:
- activations: bfloat16 [131072, 8192], P(('rows', 'inner')), may hold values from -128 to 128
- sketch_matrix: bfloat16 [8192, 256], replicated, may hold values from -0.0625 to 0.0625
- row_counts: int32 [128], P(('rows', 'inner')), may hold values from 512 to 1024, as said below
Outputs:
- basis: float32 [131072, 256], P(('rows', 'inner'))
- projected: float32 [8192, 256], P('rows')
Inputs may be any that keep to these rules, and one draw needn't show every extreme that they name: `row_counts`: some device has all 1024 slots live.
All inputs are finite; a program needn't handle non-finite values.
Results may differ from a plain program's by a relative error of at most 0.0003.
Values sent between devices are 32-bit elements; how exact they have to be, the bound alone decides.
No kernel may reach another device: no remote copies, remote signals or barrier semaphores. Data moves between devices by JAX's collectives and lax.ppermute only.
A program may use at most 128 MiB of HBM per device.

v0:
```python
import math

import jax
import jax.numpy as jnp
from jax import lax
from jax.experimental import pallas as pl
from jax.experimental.pallas import tpu as pltpu
from jax.sharding import PartitionSpec as P

SIDE = 4
BOTH = ("rows", "inner")
F32 = jnp.float32
BF16 = jnp.bfloat16
HIGH = lax.Precision.HIGHEST
NT = (((1,), (1,)), ((), ()))
TN = (((0,), (0,)), ((), ()))
GROUP = 8
PANEL = 64
AHEAD = 3
DEPTHS = (512, 1024, 1536, 1536, 1536, 1024, 512, 512)
CHUNK = 128
WIDE = 256


def device(y, x, z, core):
    return ((y % SIDE) * SIDE + x % SIDE) * 2 * SIDE + (z % SIDE) * 2 + core


def pairs(move):
    found = []
    for y in range(SIDE):
        for x in range(SIDE):
            for z in range(SIDE):
                for core in range(2):
                    found.append((device(y, x, z, core), device(*move(y, x, z, core))))
    return found


def step_on(axis, steps, y, x, z, core):
    return (y + steps * (axis == "y"), x + steps * (axis == "x"), z + steps * (axis == "z"), core)


def send(value, axes, steps):
    return lax.ppermute(value, BOTH, pairs(lambda y, x, z, core: step_on(axes[core], steps, y, x, z, core)))


def swap_cores(value):
    return lax.ppermute(value, BOTH, pairs(lambda y, x, z, core: (y, x, z, 1 - core)))


def add_partner(value, axes, partner, beside=None):
    def move(y, x, z, core):
        at = {"y": y, "x": x, "z": z}
        at[axes[core]] = partner(at[axes[core]])
        return (at["y"], at["x"], at["z"], core)

    arrived = lax.ppermute(value, BOTH, pairs(move))
    if beside is None:
        return value + arrived
    arrived, beside = lax.optimization_barrier((arrived, beside))
    return value + arrived, beside


def flip(i):
    return i ^ 1


def mirror(i):
    return SIDE - 1 - i


def sketch_kernel(place, count, act, test, held, sketch, split, gram_mine, gram_other, tests, act_sems, test_sems):
    rows, width = held.shape
    columns = sketch.shape[1]
    half = columns // 2
    copies, parts, first = [], [], 0
    for step, size in enumerate(DEPTHS):
        part = pl.ds(first, size)
        first += size
        parts.append(part)
        copies.append(
            (
                pltpu.make_async_copy(test.at[part, :], tests.at[part, :], test_sems.at[step]),
                pltpu.make_async_copy(act.at[:, part], held.at[:, part], act_sems.at[step]),
            )
        )
    for pair in copies[:AHEAD]:
        for copy in pair:
            copy.start()
    for step, (part, pair) in enumerate(zip(parts, copies)):
        for copy in pair:
            copy.wait()
        for copy in copies[step + AHEAD] if step + AHEAD < len(copies) else ():
            copy.start()
        for first in range(0, rows, CHUNK):
            here = pl.ds(first, CHUNK)
            product = jnp.dot(held[here, part], tests[part, :], preferred_element_type=F32)
            if step == 0:
                sketch[here, :] = product
            else:
                sketch[here, :] += product
    gram = jnp.zeros((columns, columns), F32)
    for first in range(0, rows, 256):
        here = pl.ds(first, 256)
        slots = lax.broadcasted_iota(jnp.int32, (256, columns), 0) + first
        live = jnp.where(slots < count[0], sketch[here, :], 0.0)
        sketch[here, :] = live
        turned = live.T
        high = turned.astype(BF16)
        split[:columns, here] = high
        split[columns:, here] = (turned - high.astype(F32)).astype(BF16)
        gram += lax.dot_general(turned, turned, NT, precision=HIGH, preferred_element_type=F32)
    core = place[4]
    upper = jnp.concatenate([gram[:half, :half], gram[: half // 2, half:]], 0)
    lower = jnp.concatenate([gram[half:, half:], gram[half // 2 : half, half:]], 0)
    gram_mine[...] = jnp.where(core == 0, upper, lower)
    gram_other[...] = jnp.where(core == 0, lower, upper)


def sketch_call(place, count, activations, sketch_matrix):
    rows, width = activations.shape
    columns = sketch_matrix.shape[1]
    packed = (columns // 2 + columns // 4, columns // 2)
    steps = len(DEPTHS)
    smem, anywhere, vmem = (pl.BlockSpec(memory_space=space) for space in (pltpu.SMEM, pltpu.HBM, pltpu.VMEM))
    return pl.pallas_call(
        sketch_kernel,
        out_shape=[
            pltpu.VMEM((rows, width), BF16),
            pltpu.VMEM((rows, columns), F32),
            pltpu.VMEM((2 * columns, rows), BF16),
            pltpu.VMEM(packed, F32),
            pltpu.VMEM(packed, F32),
        ],
        in_specs=[smem, smem, anywhere, anywhere],
        out_specs=[vmem] * 5,
        scratch_shapes=[
            pltpu.VMEM((width, columns), BF16),
            pltpu.SemaphoreType.DMA((steps,)),
            pltpu.SemaphoreType.DMA((steps,)),
        ],
        compiler_params=pltpu.CompilerParams(vmem_limit_bytes=12 * 2**20),
        cost_estimate=pl.CostEstimate(
            flops=2 * rows * width * columns, bytes_accessed=2 * width * (rows + columns), transcendentals=0
        ),
        name="sketch",
    )(place, count, *(pltpu.with_memory_space_constraint(value, pltpu.HBM) for value in (activations, sketch_matrix)))


def projection_kernel(offsets, other, place, split, held, after, *refs):
    columns = split.shape[0] // 2
    core = place[4] + other
    core = jnp.where(core == 2, 0, core)
    for i, (one, two) in enumerate(offsets):
        y = (place[0] + jnp.where(core == 0, two, one)) % SIDE
        x = (place[1] + jnp.where(core == 0, one, two)) % SIDE
        first = pl.multiple_of(((y * SIDE + x) * 2 + core) * WIDE, WIDE)
        both = jnp.dot(split[...], held[:, pl.ds(first, WIDE)], preferred_element_type=F32)
        block = both[:columns] + both[columns:]
        if other:
            refs[0][i] = block
        else:
            block = block + refs[0][i]
            refs[1 + i // SIDE][i % SIDE] = block


def projection_call(place, split, held, after, offsets, other, received=None):
    rows = held.shape[0]
    columns = split.shape[0] // 2
    smem, vmem = (pl.BlockSpec(memory_space=space) for space in (pltpu.SMEM, pltpu.VMEM))
    in_specs = [smem, vmem, vmem, pl.BlockSpec(memory_space=pl.ANY)]
    operands = [place, split, held, after]
    blocks = len(offsets)
    if other:
        out_shape = pltpu.VMEM((blocks, columns, WIDE), F32)
        out_specs = vmem
    else:
        in_specs.append(vmem)
        operands.append(received)
        out_shape = [pltpu.VMEM((SIDE, columns, WIDE), F32)] * (blocks // SIDE)
        out_specs = [vmem] * (blocks // SIDE)
    return pl.pallas_call(
        lambda *refs: projection_kernel(offsets, other, *refs),
        out_shape=out_shape,
        in_specs=in_specs,
        out_specs=out_specs,
        compiler_params=pltpu.CompilerParams(vmem_limit_bytes=8 * 2**20),
        cost_estimate=pl.CostEstimate(
            flops=4 * blocks * rows * WIDE * columns,
            bytes_accessed=blocks * 8 * WIDE * columns,
            transcendentals=0,
        ),
        name="projection",
    )(*operands)


def small_inverse(matrix):
    size = matrix.shape[0]
    groups = [matrix[first : first + GROUP, :] for first in range(0, size, GROUP)]
    lane = lax.broadcasted_iota(jnp.int32, (1, size), 1)
    sublane = lax.broadcasted_iota(jnp.int32, (GROUP, size), 0)
    for at in range(len(groups)):
        first = GROUP * at
        inside = (lane >= first) & (lane < first + GROUP)
        columns = [
            [jnp.broadcast_to(group[:, first + j : first + j + 1], (GROUP, size)) for j in range(GROUP)]
            for group in groups[at:]
        ]
        top = columns[0]
        scaled, done = [], []
        for j in range(GROUP):
            pivot = top[j][j : j + 1, :]
            reciprocal = 1.0 / pivot
            factors = [top[k][j : j + 1, :] * reciprocal for k in range(j + 1, GROUP)]
            for column in columns:
                for k, factor in enumerate(factors, j + 1):
                    column[k] = column[k] - column[j] * factor
            row = jnp.where(inside, 0.0, groups[at][j : j + 1, :])
            for i in range(j):
                row = row - top[i][j : j + 1, :] * scaled[i]
            row = jnp.where(lane == first + j, 1.0, row)
            scaled.append(row * reciprocal)
            done.append(row * lax.rsqrt(pivot))
        for below, column in enumerate(columns[1:], at + 1):
            rest = jnp.where(inside, 0.0, groups[below])
            for j in range(GROUP):
                rest = rest - column[j] * scaled[j]
            groups[below] = rest
        for j in range(GROUP):
            groups[at] = jnp.where(sublane == j, done[j], groups[at])
    rows, cols = (lax.broadcasted_iota(jnp.int32, (size, size), axis) for axis in (0, 1))
    return jnp.where(rows >= cols, jnp.concatenate(groups, 0), 0.0)


def inverse_kernel(place, mine, other, inverse, work):
    size = work.shape[0]
    half = size // 2
    core = place[4]
    upper = jnp.where(core == 0, mine[...], other[...])
    lower = jnp.where(core == 0, other[...], mine[...])
    corner = jnp.concatenate([upper[half:], lower[half:]], 0)
    work[:half, :half] = upper[:half]
    work[:half, half:] = corner
    work[half:, :half] = corner.T
    work[half:, half:] = lower[:half]
    for first in range(0, size, PANEL):
        past = first + PANEL
        rows = pl.ds(first, PANEL)
        block = small_inverse(work[rows, first:past])
        lane = lax.broadcasted_iota(jnp.int32, (PANEL, size), 1)
        parts = [jnp.zeros((PANEL, first), F32)] * (first > 0) + [block]
        parts += [jnp.zeros((PANEL, size - past), F32)] * (past < size)
        placed = jnp.concatenate(parts, 1) if len(parts) > 1 else block
        panel = jnp.dot(block, work[rows, :], precision=HIGH, preferred_element_type=F32)
        panel = jnp.where((lane >= first) & (lane < past), placed, panel)
        inverse[rows, :] = jnp.where(lane < past, panel, 0.0)
        if past < size:
            update = lax.dot_general(panel[:, past:], panel, TN, precision=HIGH, preferred_element_type=F32)
            lane = lax.broadcasted_iota(jnp.int32, (size - past, size), 1)
            old = jnp.where((lane >= first) & (lane < past), 0.0, work[past:, :])
            work[past:, :] = old - update


def vmem_call(kernel, place, operands, out_shape, scratch_shapes, flops, name):
    smem, vmem = (pl.BlockSpec(memory_space=space) for space in (pltpu.SMEM, pltpu.VMEM))
    return pl.pallas_call(
        kernel,
        out_shape=out_shape,
        in_specs=[smem] + [vmem] * len(operands),
        out_specs=jax.tree.map(lambda _: vmem, out_shape),
        scratch_shapes=scratch_shapes,
        compiler_params=pltpu.CompilerParams(vmem_limit_bytes=12 * 2**20),
        cost_estimate=pl.CostEstimate(flops=flops, bytes_accessed=4 * 2**20, transcendentals=0),
        name=name,
    )(place, *operands)


def parts_kernel(place, mine, one, two, three, *outs):
    part = outs[0].shape[0]
    for steps, out in enumerate(outs):
        here = pl.ds(pl.multiple_of(((place[2] + steps) % SIDE) * part, part), part)
        out[...] = (mine[here, :] + two[here, :]) + (one[here, :] + three[here, :])


def finish_kernel(scale, place, inverse, mine, other, projected, turned):
    columns, wide = mine.shape
    part = columns // SIDE
    core = place[4]
    for source, side in ((mine, core), (other, 1 - core)):
        for steps in range(SIDE):
            here = pl.ds(pl.multiple_of(((place[2] + SIDE - steps) % SIDE) * part, part), part)
            turned[here, :] = source[pl.ds(steps * part, part), :]
        rows = lax.dot_general(turned[...].T, inverse[...], NT, precision=HIGH, preferred_element_type=F32)
        projected[pl.ds(pl.multiple_of(side * wide, wide), wide), :] = rows * scale


def on_device(activations, sketch_matrix, row_counts):
    rows_here, width = activations.shape
    columns = sketch_matrix.shape[1]
    square = jax.ShapeDtypeStruct((columns, columns), F32)
    total_rows = rows_here * lax.axis_size(BOTH)
    row, inner = lax.axis_index("rows"), lax.axis_index("inner")
    place = jnp.stack([row // SIDE, row % SIDE, inner // 2, inner, inner % 2]).astype(jnp.int32)

    held, sketch, split, gram_mine, gram_other = sketch_call(place, row_counts, activations, sketch_matrix)

    first = [(one, two) for one in (1, 3) for two in range(SIDE)]
    second = [(one, two) for one in (2, 0) for two in range(SIDE)]
    first_far = swap_cores(projection_call(place, split, held, place, first, 1))
    packed = gram_mine + swap_cores(gram_other)
    second_far = projection_call(place, split, held, packed, second, 1)
    packed, second_far = add_partner(packed, ("x", "y"), flip, second_far)
    second_far = swap_cores(second_far)
    near = projection_call(place, split, held, packed, first, 0, first_far)
    packed, (to_one, to_three) = add_partner(packed, ("x", "y"), mirror, near)
    near = projection_call(place, split, held, packed, second, 0, second_far)
    packed, (to_two, mine) = add_partner(packed, ("y", "x"), flip, near)
    packed = add_partner(packed, ("y", "x"), mirror)
    to_one, to_three, to_two, packed = lax.optimization_barrier((to_one, to_three, to_two, packed))
    one, three = send(to_one, ("x", "y"), 1), send(to_three, ("x", "y"), 3)
    two = send(to_two, ("x", "y"), 2)
    packed = add_partner(packed, ("z", "z"), flip)
    packed = add_partner(packed, ("z", "z"), mirror)
    inverse = vmem_call(
        inverse_kernel, place, (packed, swap_cores(packed)), square, [pltpu.VMEM(square.shape, F32)],
        12 * columns**3, "inverse",
    )
    basis = lax.dot_general(sketch, inverse, NT, precision=HIGH) * math.sqrt(total_rows)

    one, two, three, inverse, basis = lax.optimization_barrier((one, two, three, inverse, basis))
    blocks = [(mine[j] + two[j]) + (one[j] + three[j]) for j in range(SIDE)]
    arrived = [send(blocks[j], ("y", "x"), j) for j in range(1, SIDE)]
    part = jax.ShapeDtypeStruct((columns // SIDE, WIDE), F32)
    parts = vmem_call(parts_kernel, place, (blocks[0], *arrived), [part] * SIDE, [], columns * WIDE, "parts")
    arrived = [send(parts[s], ("z", "z"), s) for s in range(1, SIDE)]
    total = (parts[0] + arrived[1]) + (arrived[0] + arrived[2])
    turned = jnp.concatenate([total] + [send(total, ("z", "z"), s) for s in range(1, SIDE)], 0)
    projected = vmem_call(
        lambda *refs: finish_kernel(math.sqrt(width / total_rows), *refs), place,
        (inverse, turned, swap_cores(turned)), jax.ShapeDtypeStruct((2 * WIDE, columns), F32),
        [pltpu.VMEM((columns, WIDE), F32)], 24 * columns**2 * WIDE, "finish",
    )
    return (basis, projected)


def solution(mesh):
    return jax.shard_map(
        on_device,
        mesh=mesh,
        in_specs=(P(("rows", "inner"), None), P(), P(("rows", "inner"))),
        out_specs=(P(("rows", "inner"), None), P("rows", None)),
        check_vma=False,
    )
```

profile of v0, /device:TPU:1, one launch (start us, length us, event | category | flops | bytes accessed | tf_op | source)
XLA Modules:
  0.0 101.9 jit_solution(10692387605247769851)
XLA Ops:
  1.3 0.1 stack.23.place.refs_0_.refs_3_
  1.4 10.0 %sketch.1 = (bf16[1024,8192]{1,0:T(8,128)(2,1)S(1)}, f32[1024,256]{1,0:T(8,128)S(1)}, bf16[512,1024]{1,0:T(8,128)(2,1)S(1)}, f32[192,128]{1,0:T(8,128)S(1)}, f32[192,128]{1,0:T(8,128)S(1)}) custom-call(s32[5]{0:T(128)S(1)} %stack.23.place.refs_0_.refs_3_, s32[1]{0:T(128)S(6)} %copy.5.count, bf16[1024,8192]{1,0:T(8,128)(2,1)} %act.1, bf16[8192,256]{1,0:T(8,128)(2,1)} %test.1), custom_call_target="tpu_custom_call" | custom-call | flops 4294967296 | bytes 20971520 | tf_op jit(solution)/shard_map/sketch/pallas_call | solution.py:126
  11.4 1.5 %collective-permute-start = (f32[192,128]{1,0:T(8,128)S(1)}, f32[192,128]{1,0:T(8,128)S(1)}, u32[]{:S(2)}, u32[]{:S(2)}) collective-permute-start(f32[192,128]{1,0:T(8,128)S(1)} %get-tuple-element.33), channel_id=1, source_target_pairs={{0,1},{1,0},{2,3},{3,2},{4,5},{5,4},{6,7},{7,6},{8,9},{9,8},{10,11... | collective-permute-start | bytes 294920 | tf_op jit(solution)/shard_map/ppermute | solution.py:48
  12.9 2.9 %projection.5 = f32[8,256,256]{2,1,0:T(8,128)S(1)} custom-call(s32[5]{0:T(128)S(1)} %stack.23.place.refs_0_.refs_3_, bf16[512,1024]{1,0:T(8,128)(2,1)S(1)} %get-tuple-element.34.refs_1_, bf16[1024,8192]{1,0:T(8,128)(2,1)S(1)} %get-tuple-element.35.refs_2_, s32[5]{0:T(128)S(1)} %stack.23.place.refs_0_.refs_3_), custom_call_target="tpu_custom_call" | custom-call | flops 2147483648 | bytes 4194304 | tf_op jit(solution)/shard_map/projection/pallas_call | solution.py:182
  15.8 0.1 collective-permute-start.3
  15.9 0.0 collective-permute-done
  16.0 1.5 %collective-permute-start.1 = (f32[192,128]{1,0:T(8,128)S(1)}, f32[192,128]{1,0:T(8,128)S(1)}, u32[]{:S(2)}, u32[]{:S(2)}) collective-permute-start(f32[192,128]{1,0:T(8,128)S(1)} %add.96.refs_3_), channel_id=1, source_target_pairs={{0,8},{1,33},{2,10},{3,35},{4,12},{5,37},{6,14},{7,39},{8,0},{9,41... | collective-permute-start | bytes 294920 | tf_op jit(solution)/shard_map/ppermute | solution.py:57
  17.4 2.9 %projection.4 = f32[8,256,256]{2,1,0:T(8,128)S(1)} custom-call(s32[5]{0:T(128)S(1)} %stack.23.place.refs_0_.refs_3_, bf16[512,1024]{1,0:T(8,128)(2,1)S(1)} %get-tuple-element.34.refs_1_, bf16[1024,8192]{1,0:T(8,128)(2,1)S(1)} %get-tuple-element.35.refs_2_, f32[192,128]{1,0:T(8,128)S(1)} %add.96.refs_3_), custom_call_target="tpu_custom_call" | custom-call | flops 2147483648 | bytes 4194304 | tf_op jit(solution)/shard_map/projection/pallas_call | solution.py:182
  20.3 0.0 collective-permute-done.1
  20.3 0.8 collective-permute-start.5
  21.2 3.1 %collective-permute-start.2 = (f32[192,128]{1,0:T(8,128)S(1)}, f32[192,128]{1,0:T(8,128)S(1)}, u32[]{:S(2)}, u32[]{:S(2)}) collective-permute-start(f32[192,128]{1,0:T(8,128)S(1)} %add.97.refs_3_), channel_id=1, source_target_pairs={{0,24},{1,97},{2,26},{3,99},{4,28},{5,101},{6,30},{7,103},{8,16},{... | collective-permute-start | bytes 294920 | tf_op jit(solution)/shard_map/ppermute | solution.py:57
  24.2 0.0 collective-permute-done.3.refs_4_
  24.2 2.9 %projection.6 = (f32[4,256,256]{2,1,0:T(8,128)S(1)}, f32[4,256,256]{2,1,0:T(8,128)S(1)}) custom-call(s32[5]{0:T(128)S(1)} %stack.23.place.refs_0_.refs_3_, bf16[512,1024]{1,0:T(8,128)(2,1)S(1)} %get-tuple-element.34.refs_1_, bf16[1024,8192]{1,0:T(8,128)(2,1)S(1)} %get-tuple-element.35.refs_2_, f32[192,128]{1,0:T(8,128)S(1)} %add.97.refs_3_, ...), custom_call_target="tpu_custom_call" | custom-call | flops 2147483648 | bytes 4194304 | tf_op jit(solution)/shard_map/projection/pallas_call | solution.py:182
  27.2 0.0 collective-permute-done.2
  27.2 1.3 %collective-permute-start.4 = (f32[192,128]{1,0:T(8,128)S(1)}, f32[192,128]{1,0:T(8,128)S(1)}, u32[]{:S(2)}, u32[]{:S(2)}) collective-permute-start(f32[192,128]{1,0:T(8,128)S(1)} %add.98.refs_3_), channel_id=1, source_target_pairs={{0,32},{1,9},{2,34},{3,11},{4,36},{5,13},{6,38},{7,15},{8,40},{9,1... | collective-permute-start | bytes 294920 | tf_op jit(solution)/shard_map/ppermute | solution.py:57
  28.5 2.9 %projection.7 = (f32[4,256,256]{2,1,0:T(8,128)S(1)}, f32[4,256,256]{2,1,0:T(8,128)S(1)}) custom-call(s32[5]{0:T(128)S(1)} %stack.23.place.refs_0_.refs_3_, bf16[512,1024]{1,0:T(8,128)(2,1)S(1)} %get-tuple-element.34.refs_1_, bf16[1024,8192]{1,0:T(8,128)(2,1)S(1)} %get-tuple-element.35.refs_2_, f32[192,128]{1,0:T(8,128)S(1)} %add.98.refs_3_, ...), custom_call_target="tpu_custom_call" | custom-call | flops 2147483648 | bytes 4194304 | tf_op jit(solution)/shard_map/projection/pallas_call | solution.py:182
  31.5 2.1 %collective-permute-start.6 = (f32[192,128]{1,0:T(8,128)S(1)}, f32[192,128]{1,0:T(8,128)S(1)}, u32[]{:S(2)}, u32[]{:S(2)}) collective-permute-start(f32[192,128]{1,0:T(8,128)S(1)} %add.99), channel_id=1, source_target_pairs={{0,96},{1,25},{2,98},{3,27},{4,100},{5,29},{6,102},{7,31},{8,104},... | collective-permute-start | bytes 294920 | tf_op jit(solution)/shard_map/ppermute | solution.py:57
  33.6 2.9 %collective-permute-done.6 = f32[192,128]{1,0:T(8,128)S(1)} collective-permute-done((f32[192,128]{1,0:T(8,128)S(1)}, f32[192,128]{1,0:T(8,128)S(1)}, u32[]{:S(2)}, u32[]{:S(2)}) %collective-permute-start.6) | collective-permute-done | bytes 98336 | tf_op jit(solution)/shard_map/ppermute | solution.py:57
  36.5 0.1 collective-permute-start.7
  36.6 2.6 %collective-permute-start.8 = (f32[4,256,256]{2,1,0:T(8,128)S(1)}, f32[4,256,256]{2,1,0:T(8,128)S(1)}, u32[]{:S(2)}, u32[]{:S(2)}) collective-permute-start(f32[4,256,256]{2,1,0:T(8,128)S(1)} %get-tuple-element.48), channel_id=1, source_target_pairs={{0,16},{1,65},{2,18},{3,67},{4,20},{5,69},{6,22},{7,71},{8,24},{9,... | collective-permute-start | bytes 3145736 | tf_op jit(solution)/shard_map/ppermute | solution.py:44
  39.2 0.2 collective-permute-start.9
  39.4 1.6 %collective-permute-start.10 = (f32[192,128]{1,0:T(8,128)S(1)}, f32[192,128]{1,0:T(8,128)S(1)}, u32[]{:S(2)}, u32[]{:S(2)}) collective-permute-start(f32[192,128]{1,0:T(8,128)S(1)} %add.100), channel_id=1, source_target_pairs={{0,2},{1,3},{2,0},{3,1},{4,6},{5,7},{6,4},{7,5},{8,10},{9,11},{10,... | collective-permute-start | bytes 294920 | tf_op jit(solution)/shard_map/ppermute | solution.py:57
  41.0 2.3 %collective-permute-done.10 = f32[192,128]{1,0:T(8,128)S(1)} collective-permute-done((f32[192,128]{1,0:T(8,128)S(1)}, f32[192,128]{1,0:T(8,128)S(1)}, u32[]{:S(2)}, u32[]{:S(2)}) %collective-permute-start.10) | collective-permute-done | bytes 98336 | tf_op jit(solution)/shard_map/ppermute | solution.py:57
  43.3 3.6 %collective-permute-start.11 = (f32[192,128]{1,0:T(8,128)S(1)}, f32[192,128]{1,0:T(8,128)S(1)}, u32[]{:S(2)}, u32[]{:S(2)}) collective-permute-start(f32[192,128]{1,0:T(8,128)S(1)} %add.101), channel_id=1, source_target_pairs={{0,6},{1,7},{2,4},{3,5},{4,2},{5,3},{6,0},{7,1},{8,14},{9,15},{10,... | collective-permute-start | bytes 294920 | tf_op jit(solution)/shard_map/ppermute | solution.py:57
  46.9 2.3 %collective-permute-done.11 = f32[192,128]{1,0:T(8,128)S(1)} collective-permute-done((f32[192,128]{1,0:T(8,128)S(1)}, f32[192,128]{1,0:T(8,128)S(1)}, u32[]{:S(2)}, u32[]{:S(2)}) %collective-permute-start.11) | collective-permute-done | bytes 98336 | tf_op jit(solution)/shard_map/ppermute | solution.py:57
  49.2 4.7 %collective-permute-start.12 = (f32[192,128]{1,0:T(8,128)S(1)}, f32[192,128]{1,0:T(8,128)S(1)}, u32[]{:S(2)}, u32[]{:S(2)}) collective-permute-start(f32[192,128]{1,0:T(8,128)S(1)} %add.102.mine), channel_id=1, source_target_pairs={{0,1},{1,0},{2,3},{3,2},{4,5},{5,4},{6,7},{7,6},{8,9},{9,8},{10,11... | collective-permute-start | bytes 294920 | tf_op jit(solution)/shard_map/ppermute | solution.py:48
  53.9 0.9 collective-permute-done.12.other
  54.9 8.5 %inverse.1.refs_1_ = f32[256,256]{1,0:T(8,128)S(1)} custom-call(s32[5]{0:T(128)S(1)} %stack.23.place.refs_0_.refs_3_, f32[192,128]{1,0:T(8,128)S(1)} %add.102.mine, f32[192,128]{1,0:T(8,128)S(1)} %collective-permute-done.12.other), custom_call_target="tpu_custom_call" | custom-call | flops 201326592 | bytes 4194304 | tf_op jit(solution)/shard_map/inverse/pallas_call | solution.py:266
  63.4 2.0 %convolution_multiply_fusion = f32[1024,256]{1,0:T(8,128)} fusion(f32[1024,256]{1,0:T(8,128)S(1)} %get-tuple-element.51, f32[256,256]{1,0:T(8,128)S(1)} %inverse.1.refs_1_), kind=kOutput, calls=%fused_computation | convolution fusion | flops 805568512 | bytes 2359296 | tf_op jit(solution)/shard_map/dot_general | solution.py:328
  65.4 0.3 add_bitcast_fusion
  65.6 1.6 %collective-permute-start.13 = (f32[256,256]{1,0:T(8,128)S(1)}, f32[256,256]{1,0:T(8,128)S(1)}, u32[]{:S(2)}, u32[]{:S(2)}) collective-permute-start(f32[256,256]{1,0:T(8,128)S(1)} %get-tuple-element.64), channel_id=1, source_target_pairs={{0,32},{1,9},{2,34},{3,11},{4,36},{5,13},{6,38},{7,15},{8,40},{9,1... | collective-permute-start | bytes 786440 | tf_op jit(solution)/shard_map/ppermute | solution.py:44
  67.2 2.5 %collective-permute-start.15 = (f32[256,256]{1,0:T(8,128)S(1)}, f32[256,256]{1,0:T(8,128)S(1)}, u32[]{:S(2)}, u32[]{:S(2)}) collective-permute-start(f32[256,256]{1,0:T(8,128)S(1)} %get-tuple-element.62), channel_id=1, source_target_pairs={{0,96},{1,25},{2,98},{3,27},{4,100},{5,29},{6,102},{7,31},{8,104},... | collective-permute-start | bytes 786440 | tf_op jit(solution)/shard_map/ppermute | solution.py:44
  69.7 5.5 %collective-permute-done.13.one = f32[256,256]{1,0:T(8,128)S(1)} collective-permute-done((f32[256,256]{1,0:T(8,128)S(1)}, f32[256,256]{1,0:T(8,128)S(1)}, u32[]{:S(2)}, u32[]{:S(2)}) %collective-permute-start.13) | collective-permute-done | bytes 262176 | tf_op jit(solution)/shard_map/ppermute | solution.py:44
  75.3 0.6 collective-permute-done.15.three
  75.9 0.6 parts.1
  76.5 1.6 %collective-permute-start.16 = (f32[64,256]{1,0:T(8,128)S(1)}, f32[64,256]{1,0:T(8,128)S(1)}, u32[]{:S(2)}, u32[]{:S(2)}) collective-permute-start(f32[64,256]{1,0:T(8,128)S(1)} %get-tuple-element.59), channel_id=1, source_target_pairs={{0,4},{1,5},{2,6},{3,7},{4,0},{5,1},{6,2},{7,3},{8,12},{9,13},{10,... | collective-permute-start | bytes 196616 | tf_op jit(solution)/shard_map/ppermute | solution.py:44
  78.0 2.0 %collective-permute-start.17 = (f32[64,256]{1,0:T(8,128)S(1)}, f32[64,256]{1,0:T(8,128)S(1)}, u32[]{:S(2)}, u32[]{:S(2)}) collective-permute-start(f32[64,256]{1,0:T(8,128)S(1)} %get-tuple-element.60), channel_id=1, source_target_pairs={{0,2},{1,3},{2,4},{3,5},{4,6},{5,7},{6,0},{7,1},{8,10},{9,11},{10,... | collective-permute-start | bytes 196616 | tf_op jit(solution)/shard_map/ppermute | solution.py:44
  80.1 0.7 collective-permute-start.18
  80.7 0.4 collective-permute-done.16
  81.2 1.2 %collective-permute-done.17 = f32[64,256]{1,0:T(8,128)S(1)} collective-permute-done((f32[64,256]{1,0:T(8,128)S(1)}, f32[64,256]{1,0:T(8,128)S(1)}, u32[]{:S(2)}, u32[]{:S(2)}) %collective-permute-start.17) | collective-permute-done | bytes 65568 | tf_op jit(solution)/shard_map/ppermute | solution.py:44
  82.4 0.8 collective-permute-done.18
  83.2 0.1 collective-permute-start.19
  83.3 3.0 %collective-permute-start.20 = (f32[64,256]{1,0:T(8,128)S(1)}, f32[64,256]{1,0:T(8,128)S(1)}, u32[]{:S(2)}, u32[]{:S(2)}) collective-permute-start(f32[64,256]{1,0:T(8,128)S(1)} %add_add_fusion), channel_id=1, source_target_pairs={{0,4},{1,5},{2,6},{3,7},{4,0},{5,1},{6,2},{7,3},{8,12},{9,13},{10,... | collective-permute-start | bytes 196616 | tf_op jit(solution)/shard_map/ppermute | solution.py:44
  86.3 2.9 %collective-permute-done.19 = f32[64,256]{1,0:T(8,128)S(1)} collective-permute-done((f32[64,256]{1,0:T(8,128)S(1)}, f32[64,256]{1,0:T(8,128)S(1)}, u32[]{:S(2)}, u32[]{:S(2)}) %collective-permute-start.19) | collective-permute-done | bytes 65568 | tf_op jit(solution)/shard_map/ppermute | solution.py:44
  89.2 0.2 collective-permute-done.21
  89.5 9.2 %collective-permute-start.22 = (f32[256,256]{1,0:T(8,128)S(1)}, f32[256,256]{1,0:T(8,128)S(1)}, u32[]{:S(2)}, u32[]{:S(2)}) collective-permute-start(f32[256,256]{1,0:T(8,128)S(1)} %pad_maximum_fusion.refs_2_), channel_id=1, source_target_pairs={{0,1},{1,0},{2,3},{3,2},{4,5},{5,4},{6,7},{7,6},{8,9},{9,8},{10,11... | collective-permute-start | bytes 786440 | tf_op jit(solution)/shard_map/ppermute | solution.py:48
  98.7 1.2 %collective-permute-done.22.refs_3_ = f32[256,256]{1,0:T(8,128)S(1)} collective-permute-done((f32[256,256]{1,0:T(8,128)S(1)}, f32[256,256]{1,0:T(8,128)S(1)}, u32[]{:S(2)}, u32[]{:S(2)}) %collective-permute-start.22) | collective-permute-done | bytes 262176 | tf_op jit(solution)/shard_map/ppermute | solution.py:48
  99.8 2.1 %finish.1 = f32[512,256]{1,0:T(8,128)} custom-call(s32[5]{0:T(128)S(1)} %stack.23.place.refs_0_.refs_3_, f32[256,256]{1,0:T(8,128)S(1)} %inverse.1.refs_1_, f32[256,256]{1,0:T(8,128)S(1)} %pad_maximum_fusion.refs_2_, f32[256,256]{1,0:T(8,128)S(1)} %collective-permute-done.22.refs_3_), custom_call_target="tpu_custom_call" | custom-call | flops 402653184 | bytes 4194304 | tf_op jit(solution)/shard_map/finish/pallas_call | solution.py:266
  (18 shorter events, 0.1 us)
Async XLA Ops:
  11.4 4.6 %collective-permute-start = (f32[192,128]{1,0:T(8,128)S(1)}, f32[192,128]{1,0:T(8,128)S(1)}, u32[]{:S(2)}, u32[]{:S(2)}) collective-permute-start(f32[192,128]{1,0:T(8,128)S(1)} %get-tuple-element.33), channel_id=1, source_target_pairs={{0,1},{1,0},{2,3},{3,2},{4,5},{5,4},{6,7},{7,6},{8,9},{9,8},{10,11... | collective-permute-start | bytes 294920 | tf_op jit(solution)/shard_map/ppermute | solution.py:48
  15.8 8.4 %collective-permute-start.3 = (f32[8,256,256]{2,1,0:T(8,128)S(1)}, f32[8,256,256]{2,1,0:T(8,128)S(1)}, u32[]{:S(2)}, u32[]{:S(2)}) collective-permute-start(f32[8,256,256]{2,1,0:T(8,128)S(1)} %projection.5), channel_id=1, source_target_pairs={{0,1},{1,0},{2,3},{3,2},{4,5},{5,4},{6,7},{7,6},{8,9},{9,8},{10,11... | collective-permute-start | bytes 6291464 | tf_op jit(solution)/shard_map/ppermute | solution.py:48
  16.0 4.4 %collective-permute-start.1 = (f32[192,128]{1,0:T(8,128)S(1)}, f32[192,128]{1,0:T(8,128)S(1)}, u32[]{:S(2)}, u32[]{:S(2)}) collective-permute-start(f32[192,128]{1,0:T(8,128)S(1)} %add.96.refs_3_), channel_id=1, source_target_pairs={{0,8},{1,33},{2,10},{3,35},{4,12},{5,37},{6,14},{7,39},{8,0},{9,41... | collective-permute-start | bytes 294920 | tf_op jit(solution)/shard_map/ppermute | solution.py:57
  20.3 8.1 %collective-permute-start.5 = (f32[8,256,256]{2,1,0:T(8,128)S(1)}, f32[8,256,256]{2,1,0:T(8,128)S(1)}, u32[]{:S(2)}, u32[]{:S(2)}) collective-permute-start(f32[8,256,256]{2,1,0:T(8,128)S(1)} %projection.4), channel_id=1, source_target_pairs={{0,1},{1,0},{2,3},{3,2},{4,5},{5,4},{6,7},{7,6},{8,9},{9,8},{10,11... | collective-permute-start | bytes 6291464 | tf_op jit(solution)/shard_map/ppermute | solution.py:48
  21.2 6.0 %collective-permute-start.2 = (f32[192,128]{1,0:T(8,128)S(1)}, f32[192,128]{1,0:T(8,128)S(1)}, u32[]{:S(2)}, u32[]{:S(2)}) collective-permute-start(f32[192,128]{1,0:T(8,128)S(1)} %add.97.refs_3_), channel_id=1, source_target_pairs={{0,24},{1,97},{2,26},{3,99},{4,28},{5,101},{6,30},{7,103},{8,16},{... | collective-permute-start | bytes 294920 | tf_op jit(solution)/shard_map/ppermute | solution.py:57
  27.2 4.2 %collective-permute-start.4 = (f32[192,128]{1,0:T(8,128)S(1)}, f32[192,128]{1,0:T(8,128)S(1)}, u32[]{:S(2)}, u32[]{:S(2)}) collective-permute-start(f32[192,128]{1,0:T(8,128)S(1)} %add.98.refs_3_), channel_id=1, source_target_pairs={{0,32},{1,9},{2,34},{3,11},{4,36},{5,13},{6,38},{7,15},{8,40},{9,1... | collective-permute-start | bytes 294920 | tf_op jit(solution)/shard_map/ppermute | solution.py:57
  31.5 5.1 %collective-permute-start.6 = (f32[192,128]{1,0:T(8,128)S(1)}, f32[192,128]{1,0:T(8,128)S(1)}, u32[]{:S(2)}, u32[]{:S(2)}) collective-permute-start(f32[192,128]{1,0:T(8,128)S(1)} %add.99), channel_id=1, source_target_pairs={{0,96},{1,25},{2,98},{3,27},{4,100},{5,29},{6,102},{7,31},{8,104},... | collective-permute-start | bytes 294920 | tf_op jit(solution)/shard_map/ppermute | solution.py:57
  36.5 28.8 %collective-permute-start.7 = (f32[4,256,256]{2,1,0:T(8,128)S(1)}, f32[4,256,256]{2,1,0:T(8,128)S(1)}, u32[]{:S(2)}, u32[]{:S(2)}) collective-permute-start(f32[4,256,256]{2,1,0:T(8,128)S(1)} %get-tuple-element.47), channel_id=1, source_target_pairs={{0,8},{1,33},{2,10},{3,35},{4,12},{5,37},{6,14},{7,39},{8,16},{9,4... | collective-permute-start | bytes 3145736 | tf_op jit(solution)/shard_map/ppermute | solution.py:44
  36.6 28.7 %collective-permute-start.8 = (f32[4,256,256]{2,1,0:T(8,128)S(1)}, f32[4,256,256]{2,1,0:T(8,128)S(1)}, u32[]{:S(2)}, u32[]{:S(2)}) collective-permute-start(f32[4,256,256]{2,1,0:T(8,128)S(1)} %get-tuple-element.48), channel_id=1, source_target_pairs={{0,16},{1,65},{2,18},{3,67},{4,20},{5,69},{6,22},{7,71},{8,24},{9,... | collective-permute-start | bytes 3145736 | tf_op jit(solution)/shard_map/ppermute | solution.py:44
  39.2 26.1 %collective-permute-start.9 = (f32[4,256,256]{2,1,0:T(8,128)S(1)}, f32[4,256,256]{2,1,0:T(8,128)S(1)}, u32[]{:S(2)}, u32[]{:S(2)}) collective-permute-start(f32[4,256,256]{2,1,0:T(8,128)S(1)} %get-tuple-element.49), channel_id=1, source_target_pairs={{0,24},{1,97},{2,26},{3,99},{4,28},{5,101},{6,30},{7,103},{8,0},{9... | collective-permute-start | bytes 3145736 | tf_op jit(solution)/shard_map/ppermute | solution.py:44
  39.4 3.9 %collective-permute-start.10 = (f32[192,128]{1,0:T(8,128)S(1)}, f32[192,128]{1,0:T(8,128)S(1)}, u32[]{:S(2)}, u32[]{:S(2)}) collective-permute-start(f32[192,128]{1,0:T(8,128)S(1)} %add.100), channel_id=1, source_target_pairs={{0,2},{1,3},{2,0},{3,1},{4,6},{5,7},{6,4},{7,5},{8,10},{9,11},{10,... | collective-permute-start | bytes 294920 | tf_op jit(solution)/shard_map/ppermute | solution.py:57
  43.3 5.9 %collective-permute-start.11 = (f32[192,128]{1,0:T(8,128)S(1)}, f32[192,128]{1,0:T(8,128)S(1)}, u32[]{:S(2)}, u32[]{:S(2)}) collective-permute-start(f32[192,128]{1,0:T(8,128)S(1)} %add.101), channel_id=1, source_target_pairs={{0,6},{1,7},{2,4},{3,5},{4,2},{5,3},{6,0},{7,1},{8,14},{9,15},{10,... | collective-permute-start | bytes 294920 | tf_op jit(solution)/shard_map/ppermute | solution.py:57
  49.2 5.6 %collective-permute-start.12 = (f32[192,128]{1,0:T(8,128)S(1)}, f32[192,128]{1,0:T(8,128)S(1)}, u32[]{:S(2)}, u32[]{:S(2)}) collective-permute-start(f32[192,128]{1,0:T(8,128)S(1)} %add.102.mine), channel_id=1, source_target_pairs={{0,1},{1,0},{2,3},{3,2},{4,5},{5,4},{6,7},{7,6},{8,9},{9,8},{10,11... | collective-permute-start | bytes 294920 | tf_op jit(solution)/shard_map/ppermute | solution.py:48
  65.6 9.6 %collective-permute-start.13 = (f32[256,256]{1,0:T(8,128)S(1)}, f32[256,256]{1,0:T(8,128)S(1)}, u32[]{:S(2)}, u32[]{:S(2)}) collective-permute-start(f32[256,256]{1,0:T(8,128)S(1)} %get-tuple-element.64), channel_id=1, source_target_pairs={{0,32},{1,9},{2,34},{3,11},{4,36},{5,13},{6,38},{7,15},{8,40},{9,1... | collective-permute-start | bytes 786440 | tf_op jit(solution)/shard_map/ppermute | solution.py:44
  67.2 8.0 %collective-permute-start.14 = (f32[256,256]{1,0:T(8,128)S(1)}, f32[256,256]{1,0:T(8,128)S(1)}, u32[]{:S(2)}, u32[]{:S(2)}) collective-permute-start(f32[256,256]{1,0:T(8,128)S(1)} %get-tuple-element.63), channel_id=1, source_target_pairs={{0,64},{1,17},{2,66},{3,19},{4,68},{5,21},{6,70},{7,23},{8,72},{9,... | collective-permute-start | bytes 786440 | tf_op jit(solution)/shard_map/ppermute | solution.py:44
  67.2 8.6 %collective-permute-start.15 = (f32[256,256]{1,0:T(8,128)S(1)}, f32[256,256]{1,0:T(8,128)S(1)}, u32[]{:S(2)}, u32[]{:S(2)}) collective-permute-start(f32[256,256]{1,0:T(8,128)S(1)} %get-tuple-element.62), channel_id=1, source_target_pairs={{0,96},{1,25},{2,98},{3,27},{4,100},{5,29},{6,102},{7,31},{8,104},... | collective-permute-start | bytes 786440 | tf_op jit(solution)/shard_map/ppermute | solution.py:44
  76.5 4.7 %collective-permute-start.16 = (f32[64,256]{1,0:T(8,128)S(1)}, f32[64,256]{1,0:T(8,128)S(1)}, u32[]{:S(2)}, u32[]{:S(2)}) collective-permute-start(f32[64,256]{1,0:T(8,128)S(1)} %get-tuple-element.59), channel_id=1, source_target_pairs={{0,4},{1,5},{2,6},{3,7},{4,0},{5,1},{6,2},{7,3},{8,12},{9,13},{10,... | collective-permute-start | bytes 196616 | tf_op jit(solution)/shard_map/ppermute | solution.py:44
  78.0 4.3 %collective-permute-start.17 = (f32[64,256]{1,0:T(8,128)S(1)}, f32[64,256]{1,0:T(8,128)S(1)}, u32[]{:S(2)}, u32[]{:S(2)}) collective-permute-start(f32[64,256]{1,0:T(8,128)S(1)} %get-tuple-element.60), channel_id=1, source_target_pairs={{0,2},{1,3},{2,4},{3,5},{4,6},{5,7},{6,0},{7,1},{8,10},{9,11},{10,... | collective-permute-start | bytes 196616 | tf_op jit(solution)/shard_map/ppermute | solution.py:44
  80.1 3.1 %collective-permute-start.18 = (f32[64,256]{1,0:T(8,128)S(1)}, f32[64,256]{1,0:T(8,128)S(1)}, u32[]{:S(2)}, u32[]{:S(2)}) collective-permute-start(f32[64,256]{1,0:T(8,128)S(1)} %get-tuple-element.61), channel_id=1, source_target_pairs={{0,6},{1,7},{2,0},{3,1},{4,2},{5,3},{6,4},{7,5},{8,14},{9,15},{10,... | collective-permute-start | bytes 196616 | tf_op jit(solution)/shard_map/ppermute | solution.py:44
  83.2 6.0 %collective-permute-start.19 = (f32[64,256]{1,0:T(8,128)S(1)}, f32[64,256]{1,0:T(8,128)S(1)}, u32[]{:S(2)}, u32[]{:S(2)}) collective-permute-start(f32[64,256]{1,0:T(8,128)S(1)} %add_add_fusion), channel_id=1, source_target_pairs={{0,2},{1,3},{2,4},{3,5},{4,6},{5,7},{6,0},{7,1},{8,10},{9,11},{10,... | collective-permute-start | bytes 196616 | tf_op jit(solution)/shard_map/ppermute | solution.py:44
  83.3 5.9 %collective-permute-start.20 = (f32[64,256]{1,0:T(8,128)S(1)}, f32[64,256]{1,0:T(8,128)S(1)}, u32[]{:S(2)}, u32[]{:S(2)}) collective-permute-start(f32[64,256]{1,0:T(8,128)S(1)} %add_add_fusion), channel_id=1, source_target_pairs={{0,4},{1,5},{2,6},{3,7},{4,0},{5,1},{6,2},{7,3},{8,12},{9,13},{10,... | collective-permute-start | bytes 196616 | tf_op jit(solution)/shard_map/ppermute | solution.py:44
  86.3 3.1 %collective-permute-start.21 = (f32[64,256]{1,0:T(8,128)S(1)}, f32[64,256]{1,0:T(8,128)S(1)}, u32[]{:S(2)}, u32[]{:S(2)}) collective-permute-start(f32[64,256]{1,0:T(8,128)S(1)} %add_add_fusion), channel_id=1, source_target_pairs={{0,6},{1,7},{2,0},{3,1},{4,2},{5,3},{6,4},{7,5},{8,14},{9,15},{10,... | collective-permute-start | bytes 196616 | tf_op jit(solution)/shard_map/ppermute | solution.py:44
  89.5 10.4 %collective-permute-start.22 = (f32[256,256]{1,0:T(8,128)S(1)}, f32[256,256]{1,0:T(8,128)S(1)}, u32[]{:S(2)}, u32[]{:S(2)}) collective-permute-start(f32[256,256]{1,0:T(8,128)S(1)} %pad_maximum_fusion.refs_2_), channel_id=1, source_target_pairs={{0,1},{1,0},{2,3},{3,2},{4,5},{5,4},{6,7},{7,6},{8,9},{9,8},{10,11... | collective-permute-start | bytes 786440 | tf_op jit(solution)/shard_map/ppermute | solution.py:48
where the time goes:
time: 102 us
  starting transfers between devices  43.8 us (43%)
  Pallas kernels  32.8 us (32%)
  waiting for transfers between devices  21.4 us (21%)
  matrix products  2 us (2%)
  between operations  1.47 us (1%)
    ppermute x5, starting transfers between devices, swap_cores(): lax.ppermute(value, BOTH, pairs(lambda y, x, z, core: (y, x, z, 1 - core)))  16.4 us
    ppermute x12, starting transfers between devices, send(): lax.ppermute(value, BOTH, pairs(lambda y, x, z, core: step_on(axes[core],...  14.2 us
    ppermute x6, starting transfers between devices, add_partner(): arrived = lax.ppermute(value, BOTH, pairs(move))  13.1 us
    ppermute x12, waiting for transfers between devices, send(): lax.ppermute(value, BOTH, pairs(lambda y, x, z, core: step_on(axes[core],...  11.7 us
    pallas_call x4, Pallas kernels, projection_call(): pl.pallas_call(lambda *refs: projection_kernel(offsets, other, *refs), ou...  11.7 us
    pallas_call x3, Pallas kernels, vmem_call(): pl.pallas_call(kernel, out_shape=out_shape, in_specs=[smem] + [vmem] * le...  11.1 us
    pallas_call x1, Pallas kernels, sketch_call(): pl.pallas_call(sketch_kernel, out_shape=[pltpu.VMEM((rows, width), BF16),...  9.98 us
    ppermute x6, waiting for transfers between devices, add_partner(): arrived = lax.ppermute(value, BOTH, pairs(move))  7.56 us
  transfers between devices with their start and end apart: 23, of which 12 were waited for; matrix products, arithmetic and copies ran while one was open for 2% of the time, Pallas kernels for 20%

commit v1 on v0

--- a/solution.py
+++ b/solution.py
@@ -312,27 +312,31 @@
     packed, second_far = add_partner(packed, ("x", "y"), flip, second_far)
     second_far = swap_cores(second_far)
     near = projection_call(place, split, held, packed, first, 0, first_far)
-    packed, (to_one, to_three) = add_partner(packed, ("x", "y"), mirror, near)
+    packed, near = add_partner(packed, ("x", "y"), mirror, near)
+    near, packed = lax.optimization_barrier((near, packed))
+    one, three = send(near[0], ("x", "y"), 1), send(near[1], ("x", "y"), 3)
     near = projection_call(place, split, held, packed, second, 0, second_far)
     packed, (to_two, mine) = add_partner(packed, ("y", "x"), flip, near)
-    packed = add_partner(packed, ("y", "x"), mirror)
-    to_one, to_three, to_two, packed = lax.optimization_barrier((to_one, to_three, to_two, packed))
-    one, three = send(to_one, ("x", "y"), 1), send(to_three, ("x", "y"), 3)
     two = send(to_two, ("x", "y"), 2)
     packed = add_partner(packed, ("z", "z"), flip)
     packed = add_partner(packed, ("z", "z"), mirror)
-    inverse = vmem_call(
-        inverse_kernel, place, (packed, swap_cores(packed)), square, [pltpu.VMEM(square.shape, F32)],
-        12 * columns**3, "inverse",
-    )
-    basis = lax.dot_general(sketch, inverse, NT, precision=HIGH) * math.sqrt(total_rows)
-
-    one, two, three, inverse, basis = lax.optimization_barrier((one, two, three, inverse, basis))
+    packed = add_partner(packed, ("y", "x"), mirror)
+    swapped = swap_cores(packed)
+
+    one, two, three, packed = lax.optimization_barrier((one, two, three, packed))
     blocks = [(mine[j] + two[j]) + (one[j] + three[j]) for j in range(SIDE)]
     arrived = [send(blocks[j], ("y", "x"), j) for j in range(1, SIDE)]
+    packed, swapped, blocks = lax.optimization_barrier((packed, swapped, blocks))
+    inverse = vmem_call(
+        inverse_kernel, place, (packed, swapped), square, [pltpu.VMEM(square.shape, F32)], 8 * 10**9, "inverse"
+    )
+    arrived, inverse = lax.optimization_barrier((arrived, inverse))
     part = jax.ShapeDtypeStruct((columns // SIDE, WIDE), F32)
     parts = vmem_call(parts_kernel, place, (blocks[0], *arrived), [part] * SIDE, [], columns * WIDE, "parts")
     arrived = [send(parts[s], ("z", "z"), s) for s in range(1, SIDE)]
+    inverse, mine = lax.optimization_barrier((inverse, parts[0]))
+    basis = lax.dot_general(sketch, inverse, NT, precision=HIGH) * math.sqrt(total_rows)
+    arrived, basis = lax.optimization_barrier((arrived, basis))
     total = (parts[0] + arrived[1]) + (arrived[0] + arrived[2])
     turned = jnp.concatenate([total] + [send(total, ("z", "z"), s) for s in range(1, SIDE)], 0)
     projected = vmem_call(

time: 102 us -> 94.5 us (0.926)
  starting transfers between devices: 43.8 us -> 37.5 us
  waiting for transfers between devices: 21.4 us -> 20.1 us
    ppermute x12, waiting for transfers between devices: 11.7 us -> 3.23 us  [send(): lax.ppermute(value, BOTH, pairs(lambda y, x, z, core: step_on(axes[core],...]
    ppermute x5, starting transfers between devices: 16.4 us -> 8.01 us  [swap_cores(): lax.ppermute(value, BOTH, pairs(lambda y, x, z, core: (y, x, z, 1 - core)))]
    ppermute x6, waiting for transfers between devices: 7.56 us -> 15.7 us  [add_partner(): arrived = lax.ppermute(value, BOTH, pairs(move))]
    ppermute x12, starting transfers between devices: 14.2 us -> 16.3 us  [send(): lax.ppermute(value, BOTH, pairs(lambda y, x, z, core: step_on(axes[core],...]
  transfers between devices with their start and end apart: 23 -> 23, of which waited for: 12 -> 8; matrix products, arithmetic and copies ran while one was open for 2% -> 3% of each run, Pallas kernels for 20% -> 21%
where the time goes in v1:
time: 94.5 us; the launch traced here: 94.4 us
  starting transfers between devices  37.5 us (40%)
  Pallas kernels  32.8 us (35%)
  waiting for transfers between devices  20.1 us (21%)
  matrix products  2 us (2%)
  between operations  1.47 us (2%)
    ppermute x12, starting transfers between devices, send(): lax.ppermute(value, BOTH, pairs(lambda y, x, z, core: step_on(axes[core],...  16.3 us
    ppermute x6, waiting for transfers between devices, add_partner(): arrived = lax.ppermute(value, BOTH, pairs(move))  15.7 us
    ppermute x6, starting transfers between devices, add_partner(): arrived = lax.ppermute(value, BOTH, pairs(move))  13.2 us
    pallas_call x4, Pallas kernels, projection_call(): pl.pallas_call(lambda *refs: projection_kernel(offsets, other, *refs), ou...  11.7 us
    pallas_call x3, Pallas kernels, vmem_call(): pl.pallas_call(kernel, out_shape=out_shape, in_specs=[smem] + [vmem] * le...  11.1 us
    pallas_call x1, Pallas kernels, sketch_call(): pl.pallas_call(sketch_kernel, out_shape=[pltpu.VMEM((rows, width), BF16),...  9.99 us
    ppermute x5, starting transfers between devices, swap_cores(): lax.ppermute(value, BOTH, pairs(lambda y, x, z, core: (y, x, z, 1 - core)))  8.01 us
    ppermute x12, waiting for transfers between devices, send(): lax.ppermute(value, BOTH, pairs(lambda y, x, z, core: step_on(axes[core],...  3.23 us
  transfers between devices with their start and end apart: 23, of which 8 were waited for; matrix products, arithmetic and copies ran while one was open for 3% of the time, Pallas kernels for 21%

profile of v1, /device:TPU:1, one launch (start us, length us, event | category | flops | bytes accessed | tf_op | source)
XLA Modules:
  0.0 94.4 jit_solution(12620468770476630522)
XLA Ops:
  1.3 0.1 stack.23.place.refs_0_.refs_3_
  1.4 10.0 %sketch.1 = (bf16[1024,8192]{1,0:T(8,128)(2,1)S(1)}, f32[1024,256]{1,0:T(8,128)S(1)}, bf16[512,1024]{1,0:T(8,128)(2,1)S(1)}, f32[192,128]{1,0:T(8,128)S(1)}, f32[192,128]{1,0:T(8,128)S(1)}) custom-call(s32[5]{0:T(128)S(1)} %stack.23.place.refs_0_.refs_3_, s32[1]{0:T(128)S(6)} %copy.5.count, bf16[1024,8192]{1,0:T(8,128)(2,1)} %act.1, bf16[8192,256]{1,0:T(8,128)(2,1)} %test.1), custom_call_target="tpu_custom_call" | custom-call | flops 4294967296 | bytes 20971520 | tf_op jit(solution)/shard_map/sketch/pallas_call | solution.py:126
  11.4 1.5 %collective-permute-start = (f32[192,128]{1,0:T(8,128)S(1)}, f32[192,128]{1,0:T(8,128)S(1)}, u32[]{:S(2)}, u32[]{:S(2)}) collective-permute-start(f32[192,128]{1,0:T(8,128)S(1)} %get-tuple-element.43), channel_id=1, source_target_pairs={{0,1},{1,0},{2,3},{3,2},{4,5},{5,4},{6,7},{7,6},{8,9},{9,8},{10,11... | collective-permute-start | bytes 294920 | tf_op jit(solution)/shard_map/ppermute | solution.py:48
  12.9 2.9 %projection.5 = f32[8,256,256]{2,1,0:T(8,128)S(1)} custom-call(s32[5]{0:T(128)S(1)} %stack.23.place.refs_0_.refs_3_, bf16[512,1024]{1,0:T(8,128)(2,1)S(1)} %get-tuple-element.44.refs_1_, bf16[1024,8192]{1,0:T(8,128)(2,1)S(1)} %get-tuple-element.45.refs_2_, s32[5]{0:T(128)S(1)} %stack.23.place.refs_0_.refs_3_), custom_call_target="tpu_custom_call" | custom-call | flops 2147483648 | bytes 4194304 | tf_op jit(solution)/shard_map/projection/pallas_call | solution.py:182
  15.8 0.1 collective-permute-start.3
  15.9 0.0 collective-permute-done
  16.0 1.5 %collective-permute-start.1 = (f32[192,128]{1,0:T(8,128)S(1)}, f32[192,128]{1,0:T(8,128)S(1)}, u32[]{:S(2)}, u32[]{:S(2)}) collective-permute-start(f32[192,128]{1,0:T(8,128)S(1)} %add.97.refs_3_), channel_id=1, source_target_pairs={{0,8},{1,33},{2,10},{3,35},{4,12},{5,37},{6,14},{7,39},{8,0},{9,41... | collective-permute-start | bytes 294920 | tf_op jit(solution)/shard_map/ppermute | solution.py:57
  17.4 2.9 %projection.4 = f32[8,256,256]{2,1,0:T(8,128)S(1)} custom-call(s32[5]{0:T(128)S(1)} %stack.23.place.refs_0_.refs_3_, bf16[512,1024]{1,0:T(8,128)(2,1)S(1)} %get-tuple-element.44.refs_1_, bf16[1024,8192]{1,0:T(8,128)(2,1)S(1)} %get-tuple-element.45.refs_2_, f32[192,128]{1,0:T(8,128)S(1)} %add.97.refs_3_), custom_call_target="tpu_custom_call" | custom-call | flops 2147483648 | bytes 4194304 | tf_op jit(solution)/shard_map/projection/pallas_call | solution.py:182
  20.3 0.0 collective-permute-done.1
  20.3 0.8 collective-permute-start.6
  21.2 3.1 %collective-permute-start.2 = (f32[192,128]{1,0:T(8,128)S(1)}, f32[192,128]{1,0:T(8,128)S(1)}, u32[]{:S(2)}, u32[]{:S(2)}) collective-permute-start(f32[192,128]{1,0:T(8,128)S(1)} %add.98.refs_3_), channel_id=1, source_target_pairs={{0,24},{1,97},{2,26},{3,99},{4,28},{5,101},{6,30},{7,103},{8,16},{... | collective-permute-start | bytes 294920 | tf_op jit(solution)/shard_map/ppermute | solution.py:57
  24.2 2.9 %projection.6 = (f32[4,256,256]{2,1,0:T(8,128)S(1)}, f32[4,256,256]{2,1,0:T(8,128)S(1)}) custom-call(s32[5]{0:T(128)S(1)} %stack.23.place.refs_0_.refs_3_, bf16[512,1024]{1,0:T(8,128)(2,1)S(1)} %get-tuple-element.44.refs_1_, bf16[1024,8192]{1,0:T(8,128)(2,1)S(1)} %get-tuple-element.45.refs_2_, f32[192,128]{1,0:T(8,128)S(1)} %add.98.refs_3_, ...), custom_call_target="tpu_custom_call" | custom-call | flops 2147483648 | bytes 4194304 | tf_op jit(solution)/shard_map/projection/pallas_call | solution.py:182
  27.2 1.3 %collective-permute-start.5 = (f32[192,128]{1,0:T(8,128)S(1)}, f32[192,128]{1,0:T(8,128)S(1)}, u32[]{:S(2)}, u32[]{:S(2)}) collective-permute-start(f32[192,128]{1,0:T(8,128)S(1)} %add.99.refs_3_), channel_id=1, source_target_pairs={{0,32},{1,9},{2,34},{3,11},{4,36},{5,13},{6,38},{7,15},{8,40},{9,1... | collective-permute-start | bytes 294920 | tf_op jit(solution)/shard_map/ppermute | solution.py:57
  28.5 2.7 %collective-permute-start.8 = (f32[4,256,256]{2,1,0:T(8,128)S(1)}, f32[4,256,256]{2,1,0:T(8,128)S(1)}, u32[]{:S(2)}, u32[]{:S(2)}) collective-permute-start(f32[4,256,256]{2,1,0:T(8,128)S(1)} %get-tuple-element.58), channel_id=1, source_target_pairs={{0,24},{1,97},{2,26},{3,99},{4,28},{5,101},{6,30},{7,103},{8,0},{9... | collective-permute-start | bytes 3145736 | tf_op jit(solution)/shard_map/ppermute | solution.py:44
  31.2 0.0 collective-permute-done.6.refs_4_
  31.2 2.9 %projection.7 = (f32[4,256,256]{2,1,0:T(8,128)S(1)}, f32[4,256,256]{2,1,0:T(8,128)S(1)}) custom-call(s32[5]{0:T(128)S(1)} %stack.23.place.refs_0_.refs_3_, bf16[512,1024]{1,0:T(8,128)(2,1)S(1)} %get-tuple-element.44.refs_1_, bf16[1024,8192]{1,0:T(8,128)(2,1)S(1)} %get-tuple-element.45.refs_2_, f32[192,128]{1,0:T(8,128)S(1)} %add.99.refs_3_, ...), custom_call_target="tpu_custom_call" | custom-call | flops 2147483648 | bytes 4194304 | tf_op jit(solution)/shard_map/projection/pallas_call | solution.py:182
  34.1 0.0 collective-permute-done.5
  34.1 0.3 collective-permute-start.7
  34.4 1.7 %collective-permute-start.9 = (f32[192,128]{1,0:T(8,128)S(1)}, f32[192,128]{1,0:T(8,128)S(1)}, u32[]{:S(2)}, u32[]{:S(2)}) collective-permute-start(f32[192,128]{1,0:T(8,128)S(1)} %add.100), channel_id=1, source_target_pairs={{0,2},{1,3},{2,0},{3,1},{4,6},{5,7},{6,4},{7,5},{8,10},{9,11},{10,... | collective-permute-start | bytes 294920 | tf_op jit(solution)/shard_map/ppermute | solution.py:57
  36.1 2.3 %collective-permute-done.9 = f32[192,128]{1,0:T(8,128)S(1)} collective-permute-done((f32[192,128]{1,0:T(8,128)S(1)}, f32[192,128]{1,0:T(8,128)S(1)}, u32[]{:S(2)}, u32[]{:S(2)}) %collective-permute-start.9) | collective-permute-done | bytes 98336 | tf_op jit(solution)/shard_map/ppermute | solution.py:57
  38.4 3.6 %collective-permute-start.10 = (f32[192,128]{1,0:T(8,128)S(1)}, f32[192,128]{1,0:T(8,128)S(1)}, u32[]{:S(2)}, u32[]{:S(2)}) collective-permute-start(f32[192,128]{1,0:T(8,128)S(1)} %add.101), channel_id=1, source_target_pairs={{0,6},{1,7},{2,4},{3,5},{4,2},{5,3},{6,0},{7,1},{8,14},{9,15},{10,... | collective-permute-start | bytes 294920 | tf_op jit(solution)/shard_map/ppermute | solution.py:57
  42.1 2.3 %collective-permute-done.10 = f32[192,128]{1,0:T(8,128)S(1)} collective-permute-done((f32[192,128]{1,0:T(8,128)S(1)}, f32[192,128]{1,0:T(8,128)S(1)}, u32[]{:S(2)}, u32[]{:S(2)}) %collective-permute-start.10) | collective-permute-done | bytes 98336 | tf_op jit(solution)/shard_map/ppermute | solution.py:57
  44.4 2.1 %collective-permute-start.11 = (f32[192,128]{1,0:T(8,128)S(1)}, f32[192,128]{1,0:T(8,128)S(1)}, u32[]{:S(2)}, u32[]{:S(2)}) collective-permute-start(f32[192,128]{1,0:T(8,128)S(1)} %add.102), channel_id=1, source_target_pairs={{0,96},{1,25},{2,98},{3,27},{4,100},{5,29},{6,102},{7,31},{8,104},... | collective-permute-start | bytes 294920 | tf_op jit(solution)/shard_map/ppermute | solution.py:57
  46.5 11.1 %collective-permute-done.11 = f32[192,128]{1,0:T(8,128)S(1)} collective-permute-done((f32[192,128]{1,0:T(8,128)S(1)}, f32[192,128]{1,0:T(8,128)S(1)}, u32[]{:S(2)}, u32[]{:S(2)}) %collective-permute-start.11) | collective-permute-done | bytes 98336 | tf_op jit(solution)/shard_map/ppermute | solution.py:57
  57.6 0.1 collective-permute-start.12
  57.7 0.0 collective-permute-done.4
  57.7 0.0 collective-permute-done.8
  57.7 0.3 add_bitcast_fusion
  58.0 1.2 %collective-permute-start.13 = (f32[256,256]{1,0:T(8,128)S(1)}, f32[256,256]{1,0:T(8,128)S(1)}, u32[]{:S(2)}, u32[]{:S(2)}) collective-permute-start(f32[256,256]{1,0:T(8,128)S(1)} %get-tuple-element.84), channel_id=1, source_target_pairs={{0,32},{1,9},{2,34},{3,11},{4,36},{5,13},{6,38},{7,15},{8,40},{9,1... | collective-permute-start | bytes 786440 | tf_op jit(solution)/shard_map/ppermute | solution.py:44
  59.2 2.0 %collective-permute-start.14 = (f32[256,256]{1,0:T(8,128)S(1)}, f32[256,256]{1,0:T(8,128)S(1)}, u32[]{:S(2)}, u32[]{:S(2)}) collective-permute-start(f32[256,256]{1,0:T(8,128)S(1)} %get-tuple-element.83), channel_id=1, source_target_pairs={{0,64},{1,17},{2,66},{3,19},{4,68},{5,21},{6,70},{7,23},{8,72},{9,... | collective-permute-start | bytes 786440 | tf_op jit(solution)/shard_map/ppermute | solution.py:44
  61.2 0.8 collective-permute-start.15
  62.0 8.5 %inverse.1.refs_1_ = f32[256,256]{1,0:T(8,128)S(1)} custom-call(s32[5]{0:T(128)S(1)} %stack.23.place.refs_0_.refs_3_, f32[192,128]{1,0:T(8,128)S(1)} %add.103.mine, f32[192,128]{1,0:T(8,128)S(1)} %collective-permute-done.12.other), custom_call_target="tpu_custom_call" | custom-call | flops 8000000000 | bytes 4194304 | tf_op jit(solution)/shard_map/inverse/pallas_call | solution.py:266
  70.5 0.0 collective-permute-done.13.one
  70.6 0.6 parts.1
  71.2 1.7 %collective-permute-start.16 = (f32[64,256]{1,0:T(8,128)S(1)}, f32[64,256]{1,0:T(8,128)S(1)}, u32[]{:S(2)}, u32[]{:S(2)}) collective-permute-start(f32[64,256]{1,0:T(8,128)S(1)} %get-tuple-element.71), channel_id=1, source_target_pairs={{0,2},{1,3},{2,4},{3,5},{4,6},{5,7},{6,0},{7,1},{8,10},{9,11},{10,... | collective-permute-start | bytes 196616 | tf_op jit(solution)/shard_map/ppermute | solution.py:44
  72.9 3.3 %collective-permute-start.17 = (f32[64,256]{1,0:T(8,128)S(1)}, f32[64,256]{1,0:T(8,128)S(1)}, u32[]{:S(2)}, u32[]{:S(2)}) collective-permute-start(f32[64,256]{1,0:T(8,128)S(1)} %get-tuple-element.72), channel_id=1, source_target_pairs={{0,4},{1,5},{2,6},{3,7},{4,0},{5,1},{6,2},{7,3},{8,12},{9,13},{10,... | collective-permute-start | bytes 196616 | tf_op jit(solution)/shard_map/ppermute | solution.py:44
  76.2 0.8 collective-permute-start.18
  77.0 2.0 %convolution_multiply_fusion = f32[1024,256]{1,0:T(8,128)} fusion(f32[1024,256]{1,0:T(8,128)S(1)} %get-tuple-element.74, f32[256,256]{1,0:T(8,128)S(1)} %inverse.1.refs_1_), kind=kOutput, calls=%fused_computation | convolution fusion | flops 805568512 | bytes 2359296 | tf_op jit(solution)/shard_map/dot_general | solution.py:338
  79.0 0.6 collective-permute-done.18
  79.6 0.2 collective-permute-start.19
  79.8 2.8 %collective-permute-start.20 = (f32[64,256]{1,0:T(8,128)S(1)}, f32[64,256]{1,0:T(8,128)S(1)}, u32[]{:S(2)}, u32[]{:S(2)}) collective-permute-start(f32[64,256]{1,0:T(8,128)S(1)} %add_add_fusion), channel_id=1, source_target_pairs={{0,4},{1,5},{2,6},{3,7},{4,0},{5,1},{6,2},{7,3},{8,12},{9,13},{10,... | collective-permute-start | bytes 196616 | tf_op jit(solution)/shard_map/ppermute | solution.py:44
  82.5 0.5 collective-permute-start.21
  83.1 0.9 collective-permute-done.19
  84.0 0.9 collective-permute-done.20
  84.9 0.8 collective-permute-done.21
  85.7 5.5 %collective-permute-start.22 = (f32[256,256]{1,0:T(8,128)S(1)}, f32[256,256]{1,0:T(8,128)S(1)}, u32[]{:S(2)}, u32[]{:S(2)}) collective-permute-start(f32[256,256]{1,0:T(8,128)S(1)} %pad_maximum_fusion.refs_2_), channel_id=1, source_target_pairs={{0,1},{1,0},{2,3},{3,2},{4,5},{5,4},{6,7},{7,6},{8,9},{9,8},{10,11... | collective-permute-start | bytes 786440 | tf_op jit(solution)/shard_map/ppermute | solution.py:48
  91.1 1.2 %collective-permute-done.22.refs_3_ = f32[256,256]{1,0:T(8,128)S(1)} collective-permute-done((f32[256,256]{1,0:T(8,128)S(1)}, f32[256,256]{1,0:T(8,128)S(1)}, u32[]{:S(2)}, u32[]{:S(2)}) %collective-permute-start.22) | collective-permute-done | bytes 262176 | tf_op jit(solution)/shard_map/ppermute | solution.py:48
  92.3 2.1 %finish.1 = f32[512,256]{1,0:T(8,128)} custom-call(s32[5]{0:T(128)S(1)} %stack.23.place.refs_0_.refs_3_, f32[256,256]{1,0:T(8,128)S(1)} %inverse.1.refs_1_, f32[256,256]{1,0:T(8,128)S(1)} %pad_maximum_fusion.refs_2_, f32[256,256]{1,0:T(8,128)S(1)} %collective-permute-done.22.refs_3_), custom_call_target="tpu_custom_call" | custom-call | flops 402653184 | bytes 4194304 | tf_op jit(solution)/shard_map/finish/pallas_call | solution.py:266
  (18 shorter events, 0.1 us)
Async XLA Ops:
  11.4 4.6 %collective-permute-start = (f32[192,128]{1,0:T(8,128)S(1)}, f32[192,128]{1,0:T(8,128)S(1)}, u32[]{:S(2)}, u32[]{:S(2)}) collective-permute-start(f32[192,128]{1,0:T(8,128)S(1)} %get-tuple-element.43), channel_id=1, source_target_pairs={{0,1},{1,0},{2,3},{3,2},{4,5},{5,4},{6,7},{7,6},{8,9},{9,8},{10,11... | collective-permute-start | bytes 294920 | tf_op jit(solution)/shard_map/ppermute | solution.py:48
  15.8 8.4 %collective-permute-start.3 = (f32[8,256,256]{2,1,0:T(8,128)S(1)}, f32[8,256,256]{2,1,0:T(8,128)S(1)}, u32[]{:S(2)}, u32[]{:S(2)}) collective-permute-start(f32[8,256,256]{2,1,0:T(8,128)S(1)} %projection.5), channel_id=1, source_target_pairs={{0,1},{1,0},{2,3},{3,2},{4,5},{5,4},{6,7},{7,6},{8,9},{9,8},{10,11... | collective-permute-start | bytes 6291464 | tf_op jit(solution)/shard_map/ppermute | solution.py:48
  16.0 4.4 %collective-permute-start.1 = (f32[192,128]{1,0:T(8,128)S(1)}, f32[192,128]{1,0:T(8,128)S(1)}, u32[]{:S(2)}, u32[]{:S(2)}) collective-permute-start(f32[192,128]{1,0:T(8,128)S(1)} %add.97.refs_3_), channel_id=1, source_target_pairs={{0,8},{1,33},{2,10},{3,35},{4,12},{5,37},{6,14},{7,39},{8,0},{9,41... | collective-permute-start | bytes 294920 | tf_op jit(solution)/shard_map/ppermute | solution.py:57
  20.3 10.8 %collective-permute-start.6 = (f32[8,256,256]{2,1,0:T(8,128)S(1)}, f32[8,256,256]{2,1,0:T(8,128)S(1)}, u32[]{:S(2)}, u32[]{:S(2)}) collective-permute-start(f32[8,256,256]{2,1,0:T(8,128)S(1)} %projection.4), channel_id=1, source_target_pairs={{0,1},{1,0},{2,3},{3,2},{4,5},{5,4},{6,7},{7,6},{8,9},{9,8},{10,11... | collective-permute-start | bytes 6291464 | tf_op jit(solution)/shard_map/ppermute | solution.py:48
  21.2 6.0 %collective-permute-start.2 = (f32[192,128]{1,0:T(8,128)S(1)}, f32[192,128]{1,0:T(8,128)S(1)}, u32[]{:S(2)}, u32[]{:S(2)}) collective-permute-start(f32[192,128]{1,0:T(8,128)S(1)} %add.98.refs_3_), channel_id=1, source_target_pairs={{0,24},{1,97},{2,26},{3,99},{4,28},{5,101},{6,30},{7,103},{8,16},{... | collective-permute-start | bytes 294920 | tf_op jit(solution)/shard_map/ppermute | solution.py:57
  27.2 6.9 %collective-permute-start.5 = (f32[192,128]{1,0:T(8,128)S(1)}, f32[192,128]{1,0:T(8,128)S(1)}, u32[]{:S(2)}, u32[]{:S(2)}) collective-permute-start(f32[192,128]{1,0:T(8,128)S(1)} %add.99.refs_3_), channel_id=1, source_target_pairs={{0,32},{1,9},{2,34},{3,11},{4,36},{5,13},{6,38},{7,15},{8,40},{9,1... | collective-permute-start | bytes 294920 | tf_op jit(solution)/shard_map/ppermute | solution.py:57
  28.5 29.2 %collective-permute-start.4 = (f32[4,256,256]{2,1,0:T(8,128)S(1)}, f32[4,256,256]{2,1,0:T(8,128)S(1)}, u32[]{:S(2)}, u32[]{:S(2)}) collective-permute-start(f32[4,256,256]{2,1,0:T(8,128)S(1)} %get-tuple-element.52), channel_id=1, source_target_pairs={{0,8},{1,33},{2,10},{3,35},{4,12},{5,37},{6,14},{7,39},{8,16},{9,4... | collective-permute-start | bytes 3145736 | tf_op jit(solution)/shard_map/ppermute | solution.py:44
  28.5 29.2 %collective-permute-start.8 = (f32[4,256,256]{2,1,0:T(8,128)S(1)}, f32[4,256,256]{2,1,0:T(8,128)S(1)}, u32[]{:S(2)}, u32[]{:S(2)}) collective-permute-start(f32[4,256,256]{2,1,0:T(8,128)S(1)} %get-tuple-element.58), channel_id=1, source_target_pairs={{0,24},{1,97},{2,26},{3,99},{4,28},{5,101},{6,30},{7,103},{8,0},{9... | collective-permute-start | bytes 3145736 | tf_op jit(solution)/shard_map/ppermute | solution.py:44
  34.1 23.6 %collective-permute-start.7 = (f32[4,256,256]{2,1,0:T(8,128)S(1)}, f32[4,256,256]{2,1,0:T(8,128)S(1)}, u32[]{:S(2)}, u32[]{:S(2)}) collective-permute-start(f32[4,256,256]{2,1,0:T(8,128)S(1)} %get-tuple-element.57), channel_id=1, source_target_pairs={{0,16},{1,65},{2,18},{3,67},{4,20},{5,69},{6,22},{7,71},{8,24},{9,... | collective-permute-start | bytes 3145736 | tf_op jit(solution)/shard_map/ppermute | solution.py:44
  34.4 4.0 %collective-permute-start.9 = (f32[192,128]{1,0:T(8,128)S(1)}, f32[192,128]{1,0:T(8,128)S(1)}, u32[]{:S(2)}, u32[]{:S(2)}) collective-permute-start(f32[192,128]{1,0:T(8,128)S(1)} %add.100), channel_id=1, source_target_pairs={{0,2},{1,3},{2,0},{3,1},{4,6},{5,7},{6,4},{7,5},{8,10},{9,11},{10,... | collective-permute-start | bytes 294920 | tf_op jit(solution)/shard_map/ppermute | solution.py:57
  38.4 5.9 %collective-permute-start.10 = (f32[192,128]{1,0:T(8,128)S(1)}, f32[192,128]{1,0:T(8,128)S(1)}, u32[]{:S(2)}, u32[]{:S(2)}) collective-permute-start(f32[192,128]{1,0:T(8,128)S(1)} %add.101), channel_id=1, source_target_pairs={{0,6},{1,7},{2,4},{3,5},{4,2},{5,3},{6,0},{7,1},{8,14},{9,15},{10,... | collective-permute-start | bytes 294920 | tf_op jit(solution)/shard_map/ppermute | solution.py:57
  44.4 13.2 %collective-permute-start.11 = (f32[192,128]{1,0:T(8,128)S(1)}, f32[192,128]{1,0:T(8,128)S(1)}, u32[]{:S(2)}, u32[]{:S(2)}) collective-permute-start(f32[192,128]{1,0:T(8,128)S(1)} %add.102), channel_id=1, source_target_pairs={{0,96},{1,25},{2,98},{3,27},{4,100},{5,29},{6,102},{7,31},{8,104},... | collective-permute-start | bytes 294920 | tf_op jit(solution)/shard_map/ppermute | solution.py:57
  57.6 4.5 %collective-permute-start.12 = (f32[192,128]{1,0:T(8,128)S(1)}, f32[192,128]{1,0:T(8,128)S(1)}, u32[]{:S(2)}, u32[]{:S(2)}) collective-permute-start(f32[192,128]{1,0:T(8,128)S(1)} %add.103.mine), channel_id=1, source_target_pairs={{0,1},{1,0},{2,3},{3,2},{4,5},{5,4},{6,7},{7,6},{8,9},{9,8},{10,11... | collective-permute-start | bytes 294920 | tf_op jit(solution)/shard_map/ppermute | solution.py:48
  58.0 12.5 %collective-permute-start.13 = (f32[256,256]{1,0:T(8,128)S(1)}, f32[256,256]{1,0:T(8,128)S(1)}, u32[]{:S(2)}, u32[]{:S(2)}) collective-permute-start(f32[256,256]{1,0:T(8,128)S(1)} %get-tuple-element.84), channel_id=1, source_target_pairs={{0,32},{1,9},{2,34},{3,11},{4,36},{5,13},{6,38},{7,15},{8,40},{9,1... | collective-permute-start | bytes 786440 | tf_op jit(solution)/shard_map/ppermute | solution.py:44
  59.2 11.3 %collective-permute-start.14 = (f32[256,256]{1,0:T(8,128)S(1)}, f32[256,256]{1,0:T(8,128)S(1)}, u32[]{:S(2)}, u32[]{:S(2)}) collective-permute-start(f32[256,256]{1,0:T(8,128)S(1)} %get-tuple-element.83), channel_id=1, source_target_pairs={{0,64},{1,17},{2,66},{3,19},{4,68},{5,21},{6,70},{7,23},{8,72},{9,... | collective-permute-start | bytes 786440 | tf_op jit(solution)/shard_map/ppermute | solution.py:44
  61.2 9.3 %collective-permute-start.15 = (f32[256,256]{1,0:T(8,128)S(1)}, f32[256,256]{1,0:T(8,128)S(1)}, u32[]{:S(2)}, u32[]{:S(2)}) collective-permute-start(f32[256,256]{1,0:T(8,128)S(1)} %get-tuple-element.82), channel_id=1, source_target_pairs={{0,96},{1,25},{2,98},{3,27},{4,100},{5,29},{6,102},{7,31},{8,104},... | collective-permute-start | bytes 786440 | tf_op jit(solution)/shard_map/ppermute | solution.py:44
  71.2 7.8 %collective-permute-start.16 = (f32[64,256]{1,0:T(8,128)S(1)}, f32[64,256]{1,0:T(8,128)S(1)}, u32[]{:S(2)}, u32[]{:S(2)}) collective-permute-start(f32[64,256]{1,0:T(8,128)S(1)} %get-tuple-element.71), channel_id=1, source_target_pairs={{0,2},{1,3},{2,4},{3,5},{4,6},{5,7},{6,0},{7,1},{8,10},{9,11},{10,... | collective-permute-start | bytes 196616 | tf_op jit(solution)/shard_map/ppermute | solution.py:44
  72.9 6.1 %collective-permute-start.17 = (f32[64,256]{1,0:T(8,128)S(1)}, f32[64,256]{1,0:T(8,128)S(1)}, u32[]{:S(2)}, u32[]{:S(2)}) collective-permute-start(f32[64,256]{1,0:T(8,128)S(1)} %get-tuple-element.72), channel_id=1, source_target_pairs={{0,4},{1,5},{2,6},{3,7},{4,0},{5,1},{6,2},{7,3},{8,12},{9,13},{10,... | collective-permute-start | bytes 196616 | tf_op jit(solution)/shard_map/ppermute | solution.py:44
  76.2 3.4 %collective-permute-start.18 = (f32[64,256]{1,0:T(8,128)S(1)}, f32[64,256]{1,0:T(8,128)S(1)}, u32[]{:S(2)}, u32[]{:S(2)}) collective-permute-start(f32[64,256]{1,0:T(8,128)S(1)} %get-tuple-element.73), channel_id=1, source_target_pairs={{0,6},{1,7},{2,0},{3,1},{4,2},{5,3},{6,4},{7,5},{8,14},{9,15},{10,... | collective-permute-start | bytes 196616 | tf_op jit(solution)/shard_map/ppermute | solution.py:44
  79.6 4.4 %collective-permute-start.19 = (f32[64,256]{1,0:T(8,128)S(1)}, f32[64,256]{1,0:T(8,128)S(1)}, u32[]{:S(2)}, u32[]{:S(2)}) collective-permute-start(f32[64,256]{1,0:T(8,128)S(1)} %add_add_fusion), channel_id=1, source_target_pairs={{0,2},{1,3},{2,4},{3,5},{4,6},{5,7},{6,0},{7,1},{8,10},{9,11},{10,... | collective-permute-start | bytes 196616 | tf_op jit(solution)/shard_map/ppermute | solution.py:44
  79.8 5.1 %collective-permute-start.20 = (f32[64,256]{1,0:T(8,128)S(1)}, f32[64,256]{1,0:T(8,128)S(1)}, u32[]{:S(2)}, u32[]{:S(2)}) collective-permute-start(f32[64,256]{1,0:T(8,128)S(1)} %add_add_fusion), channel_id=1, source_target_pairs={{0,4},{1,5},{2,6},{3,7},{4,0},{5,1},{6,2},{7,3},{8,12},{9,13},{10,... | collective-permute-start | bytes 196616 | tf_op jit(solution)/shard_map/ppermute | solution.py:44
  82.5 3.1 %collective-permute-start.21 = (f32[64,256]{1,0:T(8,128)S(1)}, f32[64,256]{1,0:T(8,128)S(1)}, u32[]{:S(2)}, u32[]{:S(2)}) collective-permute-start(f32[64,256]{1,0:T(8,128)S(1)} %add_add_fusion), channel_id=1, source_target_pairs={{0,6},{1,7},{2,0},{3,1},{4,2},{5,3},{6,4},{7,5},{8,14},{9,15},{10,... | collective-permute-start | bytes 196616 | tf_op jit(solution)/shard_map/ppermute | solution.py:44
  85.7 6.6 %collective-permute-start.22 = (f32[256,256]{1,0:T(8,128)S(1)}, f32[256,256]{1,0:T(8,128)S(1)}, u32[]{:S(2)}, u32[]{:S(2)}) collective-permute-start(f32[256,256]{1,0:T(8,128)S(1)} %pad_maximum_fusion.refs_2_), channel_id=1, source_target_pairs={{0,1},{1,0},{2,3},{3,2},{4,5},{5,4},{6,7},{7,6},{8,9},{9,8},{10,11... | collective-permute-start | bytes 786440 | tf_op jit(solution)/shard_map/ppermute | solution.py:48

commit v2 on v1

--- a/solution.py
+++ b/solution.py
@@ -275,22 +275,11 @@
     )(place, *operands)
 
 
-def parts_kernel(place, mine, one, two, three, *outs):
-    part = outs[0].shape[0]
-    for steps, out in enumerate(outs):
-        here = pl.ds(pl.multiple_of(((place[2] + steps) % SIDE) * part, part), part)
-        out[...] = (mine[here, :] + two[here, :]) + (one[here, :] + three[here, :])
-
-
-def finish_kernel(scale, place, inverse, mine, other, projected, turned):
-    columns, wide = mine.shape
-    part = columns // SIDE
+def finish_kernel(scale, place, inverse, mine, other, projected):
+    wide = mine.shape[1]
     core = place[4]
     for source, side in ((mine, core), (other, 1 - core)):
-        for steps in range(SIDE):
-            here = pl.ds(pl.multiple_of(((place[2] + SIDE - steps) % SIDE) * part, part), part)
-            turned[here, :] = source[pl.ds(steps * part, part), :]
-        rows = lax.dot_general(turned[...].T, inverse[...], NT, precision=HIGH, preferred_element_type=F32)
+        rows = lax.dot_general(source[...].T, inverse[...], NT, precision=HIGH, preferred_element_type=F32)
         projected[pl.ds(pl.multiple_of(side * wide, wide), wide), :] = rows * scale
 
 
@@ -300,7 +289,7 @@
     square = jax.ShapeDtypeStruct((columns, columns), F32)
     total_rows = rows_here * lax.axis_size(BOTH)
     row, inner = lax.axis_index("rows"), lax.axis_index("inner")
-    place = jnp.stack([row // SIDE, row % SIDE, inner // 2, inner, inner % 2]).astype(jnp.int32)
+    place = jnp.stack([row >> 2, row & 3, inner >> 1, inner, inner & 1]).astype(jnp.int32)
 
     held, sketch, split, gram_mine, gram_other = sketch_call(place, row_counts, activations, sketch_matrix)
 
@@ -320,29 +309,26 @@
     two = send(to_two, ("x", "y"), 2)
     packed = add_partner(packed, ("z", "z"), flip)
     packed = add_partner(packed, ("z", "z"), mirror)
+
     packed = add_partner(packed, ("y", "x"), mirror)
     swapped = swap_cores(packed)
 
     one, two, three, packed = lax.optimization_barrier((one, two, three, packed))
     blocks = [(mine[j] + two[j]) + (one[j] + three[j]) for j in range(SIDE)]
     arrived = [send(blocks[j], ("y", "x"), j) for j in range(1, SIDE)]
-    packed, swapped, blocks = lax.optimization_barrier((packed, swapped, blocks))
+    block = (blocks[0] + arrived[1]) + (arrived[0] + arrived[2])
+    packed, swapped, block = lax.optimization_barrier((packed, swapped, block))
+    arrived = [send(block, ("z", "z"), s) for s in range(1, SIDE)]
     inverse = vmem_call(
         inverse_kernel, place, (packed, swapped), square, [pltpu.VMEM(square.shape, F32)], 8 * 10**9, "inverse"
     )
-    arrived, inverse = lax.optimization_barrier((arrived, inverse))
-    part = jax.ShapeDtypeStruct((columns // SIDE, WIDE), F32)
-    parts = vmem_call(parts_kernel, place, (blocks[0], *arrived), [part] * SIDE, [], columns * WIDE, "parts")
-    arrived = [send(parts[s], ("z", "z"), s) for s in range(1, SIDE)]
-    inverse, mine = lax.optimization_barrier((inverse, parts[0]))
     basis = lax.dot_general(sketch, inverse, NT, precision=HIGH) * math.sqrt(total_rows)
     arrived, basis = lax.optimization_barrier((arrived, basis))
-    total = (parts[0] + arrived[1]) + (arrived[0] + arrived[2])
-    turned = jnp.concatenate([total] + [send(total, ("z", "z"), s) for s in range(1, SIDE)], 0)
+    block = (block + arrived[1]) + (arrived[0] + arrived[2])
     projected = vmem_call(
         lambda *refs: finish_kernel(math.sqrt(width / total_rows), *refs), place,
-        (inverse, turned, swap_cores(turned)), jax.ShapeDtypeStruct((2 * WIDE, columns), F32),
-        [pltpu.VMEM((columns, WIDE), F32)], 24 * columns**2 * WIDE, "finish",
+        (inverse, block, swap_cores(block)), jax.ShapeDtypeStruct((2 * WIDE, columns), F32),
+        [], 24 * columns**2 * WIDE, "finish",
     )
     return (basis, projected)
 

time: 94.5 us -> 89.2 us (0.944)
  starting transfers between devices: 37.5 us -> 32 us
    ppermute x12 -> x9, starting transfers between devices: 16.3 us -> 12.5 us  [send(): lax.ppermute(value, BOTH, pairs(lambda y, x, z, core: step_on(axes[core],...]
    ppermute x5, starting transfers between devices: 8.01 us -> 6.4 us  [swap_cores(): lax.ppermute(value, BOTH, pairs(lambda y, x, z, core: (y, x, z, 1 - core)))]
    ppermute x12 -> x9, waiting for transfers between devices: 3.23 us -> 4.01 us  [send(): lax.ppermute(value, BOTH, pairs(lambda y, x, z, core: step_on(axes[core],...]
    pallas_call x3 -> x2, Pallas kernels: 11.1 us -> 10.5 us  [vmem_call(): pl.pallas_call(kernel, out_shape=out_shape, in_specs=[smem] + [vmem] * le...]
  transfers between devices with their start and end apart: 23 -> 20, of which waited for: 8 -> 6; matrix products, arithmetic and copies ran while one was open for 3% -> 2% of each run, Pallas kernels for 21% -> 23%
where the time goes in v2:
time: 89.2 us; the launch traced here: 89.1 us
  Pallas kernels  32.2 us (36%)
  starting transfers between devices  32 us (36%)
  waiting for transfers between devices  20.9 us (23%)
  matrix products  2 us (2%)
  between operations  1.44 us (2%)
    ppermute x6, waiting for transfers between devices, add_partner(): arrived = lax.ppermute(value, BOTH, pairs(move))  15.7 us
    ppermute x6, starting transfers between devices, add_partner(): arrived = lax.ppermute(value, BOTH, pairs(move))  13.1 us
    ppermute x9, starting transfers between devices, send(): lax.ppermute(value, BOTH, pairs(lambda y, x, z, core: step_on(axes[core],...  12.5 us
    pallas_call x4, Pallas kernels, projection_call(): pl.pallas_call(lambda *refs: projection_kernel(offsets, other, *refs), ou...  11.7 us
    pallas_call x2, Pallas kernels, vmem_call(): pl.pallas_call(kernel, out_shape=out_shape, in_specs=[smem] + [vmem] * le...  10.5 us
    pallas_call x1, Pallas kernels, sketch_call(): pl.pallas_call(sketch_kernel, out_shape=[pltpu.VMEM((rows, width), BF16),...  10 us
    ppermute x5, starting transfers between devices, swap_cores(): lax.ppermute(value, BOTH, pairs(lambda y, x, z, core: (y, x, z, 1 - core)))  6.4 us
    ppermute x9, waiting for transfers between devices, send(): lax.ppermute(value, BOTH, pairs(lambda y, x, z, core: step_on(axes[core],...  4.01 us
  transfers between devices with their start and end apart: 20, of which 6 were waited for; matrix products, arithmetic and copies ran while one was open for 2% of the time, Pallas kernels for 23%

profile of v2, /device:TPU:1, one launch (start us, length us, event | category | flops | bytes accessed | tf_op | source)
XLA Modules:
  0.0 89.1 jit_solution(4188365939254986664)
XLA Ops:
  1.3 0.1 stack.23.place.refs_0_.refs_3_
  1.4 10.0 %sketch.1 = (bf16[1024,8192]{1,0:T(8,128)(2,1)S(1)}, f32[1024,256]{1,0:T(8,128)S(1)}, bf16[512,1024]{1,0:T(8,128)(2,1)S(1)}, f32[192,128]{1,0:T(8,128)S(1)}, f32[192,128]{1,0:T(8,128)S(1)}) custom-call(s32[5]{0:T(128)S(1)} %stack.23.place.refs_0_.refs_3_, s32[1]{0:T(128)S(6)} %copy.5.count, bf16[1024,8192]{1,0:T(8,128)(2,1)} %act.1, bf16[8192,256]{1,0:T(8,128)(2,1)} %test.1), custom_call_target="tpu_custom_call" | custom-call | flops 4294967296 | bytes 20971520 | tf_op jit(solution)/shard_map/sketch/pallas_call | solution.py:126
  11.4 1.5 %collective-permute-start = (f32[192,128]{1,0:T(8,128)S(1)}, f32[192,128]{1,0:T(8,128)S(1)}, u32[]{:S(2)}, u32[]{:S(2)}) collective-permute-start(f32[192,128]{1,0:T(8,128)S(1)} %get-tuple-element.34), channel_id=1, source_target_pairs={{0,1},{1,0},{2,3},{3,2},{4,5},{5,4},{6,7},{7,6},{8,9},{9,8},{10,11... | collective-permute-start | bytes 294920 | tf_op jit(solution)/shard_map/ppermute | solution.py:48
  12.9 2.9 %projection.5 = f32[8,256,256]{2,1,0:T(8,128)S(1)} custom-call(s32[5]{0:T(128)S(1)} %stack.23.place.refs_0_.refs_3_, bf16[512,1024]{1,0:T(8,128)(2,1)S(1)} %get-tuple-element.35.refs_1_, bf16[1024,8192]{1,0:T(8,128)(2,1)S(1)} %get-tuple-element.36.refs_2_, s32[5]{0:T(128)S(1)} %stack.23.place.refs_0_.refs_3_), custom_call_target="tpu_custom_call" | custom-call | flops 2147483648 | bytes 4194304 | tf_op jit(solution)/shard_map/projection/pallas_call | solution.py:182
  15.8 0.1 collective-permute-start.3
  15.9 0.0 collective-permute-done
  15.9 1.4 %collective-permute-start.1 = (f32[192,128]{1,0:T(8,128)S(1)}, f32[192,128]{1,0:T(8,128)S(1)}, u32[]{:S(2)}, u32[]{:S(2)}) collective-permute-start(f32[192,128]{1,0:T(8,128)S(1)} %add.95.refs_3_), channel_id=1, source_target_pairs={{0,8},{1,33},{2,10},{3,35},{4,12},{5,37},{6,14},{7,39},{8,0},{9,41... | collective-permute-start | bytes 294920 | tf_op jit(solution)/shard_map/ppermute | solution.py:57
  17.4 2.9 %projection.4 = f32[8,256,256]{2,1,0:T(8,128)S(1)} custom-call(s32[5]{0:T(128)S(1)} %stack.23.place.refs_0_.refs_3_, bf16[512,1024]{1,0:T(8,128)(2,1)S(1)} %get-tuple-element.35.refs_1_, bf16[1024,8192]{1,0:T(8,128)(2,1)S(1)} %get-tuple-element.36.refs_2_, f32[192,128]{1,0:T(8,128)S(1)} %add.95.refs_3_), custom_call_target="tpu_custom_call" | custom-call | flops 2147483648 | bytes 4194304 | tf_op jit(solution)/shard_map/projection/pallas_call | solution.py:182
  20.3 0.0 collective-permute-done.1
  20.3 0.9 collective-permute-start.6
  21.1 3.0 %collective-permute-start.2 = (f32[192,128]{1,0:T(8,128)S(1)}, f32[192,128]{1,0:T(8,128)S(1)}, u32[]{:S(2)}, u32[]{:S(2)}) collective-permute-start(f32[192,128]{1,0:T(8,128)S(1)} %add.96.refs_3_), channel_id=1, source_target_pairs={{0,24},{1,97},{2,26},{3,99},{4,28},{5,101},{6,30},{7,103},{8,16},{... | collective-permute-start | bytes 294920 | tf_op jit(solution)/shard_map/ppermute | solution.py:57
  24.2 0.0 collective-permute-done.3.refs_4_
  24.2 2.9 %projection.6 = (f32[4,256,256]{2,1,0:T(8,128)S(1)}, f32[4,256,256]{2,1,0:T(8,128)S(1)}) custom-call(s32[5]{0:T(128)S(1)} %stack.23.place.refs_0_.refs_3_, bf16[512,1024]{1,0:T(8,128)(2,1)S(1)} %get-tuple-element.35.refs_1_, bf16[1024,8192]{1,0:T(8,128)(2,1)S(1)} %get-tuple-element.36.refs_2_, f32[192,128]{1,0:T(8,128)S(1)} %add.96.refs_3_, ...), custom_call_target="tpu_custom_call" | custom-call | flops 2147483648 | bytes 4194304 | tf_op jit(solution)/shard_map/projection/pallas_call | solution.py:182
  27.1 0.0 collective-permute-done.2
  27.1 1.2 %collective-permute-start.5 = (f32[192,128]{1,0:T(8,128)S(1)}, f32[192,128]{1,0:T(8,128)S(1)}, u32[]{:S(2)}, u32[]{:S(2)}) collective-permute-start(f32[192,128]{1,0:T(8,128)S(1)} %add.97.refs_3_), channel_id=1, source_target_pairs={{0,32},{1,9},{2,34},{3,11},{4,36},{5,13},{6,38},{7,15},{8,40},{9,1... | collective-permute-start | bytes 294920 | tf_op jit(solution)/shard_map/ppermute | solution.py:57
  28.4 0.0 collective-permute-start.4
  28.4 2.7 %collective-permute-start.8 = (f32[4,256,256]{2,1,0:T(8,128)S(1)}, f32[4,256,256]{2,1,0:T(8,128)S(1)}, u32[]{:S(2)}, u32[]{:S(2)}) collective-permute-start(f32[4,256,256]{2,1,0:T(8,128)S(1)} %get-tuple-element.49), channel_id=1, source_target_pairs={{0,24},{1,97},{2,26},{3,99},{4,28},{5,101},{6,30},{7,103},{8,0},{9... | collective-permute-start | bytes 3145736 | tf_op jit(solution)/shard_map/ppermute | solution.py:44
  31.1 2.9 %projection.7 = (f32[4,256,256]{2,1,0:T(8,128)S(1)}, f32[4,256,256]{2,1,0:T(8,128)S(1)}) custom-call(s32[5]{0:T(128)S(1)} %stack.23.place.refs_0_.refs_3_, bf16[512,1024]{1,0:T(8,128)(2,1)S(1)} %get-tuple-element.35.refs_1_, bf16[1024,8192]{1,0:T(8,128)(2,1)S(1)} %get-tuple-element.36.refs_2_, f32[192,128]{1,0:T(8,128)S(1)} %add.97.refs_3_, ...), custom_call_target="tpu_custom_call" | custom-call | flops 2147483648 | bytes 4194304 | tf_op jit(solution)/shard_map/projection/pallas_call | solution.py:182
  34.0 0.3 collective-permute-start.7
  34.4 1.7 %collective-permute-start.9 = (f32[192,128]{1,0:T(8,128)S(1)}, f32[192,128]{1,0:T(8,128)S(1)}, u32[]{:S(2)}, u32[]{:S(2)}) collective-permute-start(f32[192,128]{1,0:T(8,128)S(1)} %add.98), channel_id=1, source_target_pairs={{0,2},{1,3},{2,0},{3,1},{4,6},{5,7},{6,4},{7,5},{8,10},{9,11},{10,... | collective-permute-start | bytes 294920 | tf_op jit(solution)/shard_map/ppermute | solution.py:57
  36.1 2.3 %collective-permute-done.9 = f32[192,128]{1,0:T(8,128)S(1)} collective-permute-done((f32[192,128]{1,0:T(8,128)S(1)}, f32[192,128]{1,0:T(8,128)S(1)}, u32[]{:S(2)}, u32[]{:S(2)}) %collective-permute-start.9) | collective-permute-done | bytes 98336 | tf_op jit(solution)/shard_map/ppermute | solution.py:57
  38.4 3.7 %collective-permute-start.10 = (f32[192,128]{1,0:T(8,128)S(1)}, f32[192,128]{1,0:T(8,128)S(1)}, u32[]{:S(2)}, u32[]{:S(2)}) collective-permute-start(f32[192,128]{1,0:T(8,128)S(1)} %add.99), channel_id=1, source_target_pairs={{0,6},{1,7},{2,4},{3,5},{4,2},{5,3},{6,0},{7,1},{8,14},{9,15},{10,... | collective-permute-start | bytes 294920 | tf_op jit(solution)/shard_map/ppermute | solution.py:57
  42.1 2.3 %collective-permute-done.10 = f32[192,128]{1,0:T(8,128)S(1)} collective-permute-done((f32[192,128]{1,0:T(8,128)S(1)}, f32[192,128]{1,0:T(8,128)S(1)}, u32[]{:S(2)}, u32[]{:S(2)}) %collective-permute-start.10) | collective-permute-done | bytes 98336 | tf_op jit(solution)/shard_map/ppermute | solution.py:57
  44.4 2.0 %collective-permute-start.11 = (f32[192,128]{1,0:T(8,128)S(1)}, f32[192,128]{1,0:T(8,128)S(1)}, u32[]{:S(2)}, u32[]{:S(2)}) collective-permute-start(f32[192,128]{1,0:T(8,128)S(1)} %add.100), channel_id=1, source_target_pairs={{0,96},{1,25},{2,98},{3,27},{4,100},{5,29},{6,102},{7,31},{8,104},... | collective-permute-start | bytes 294920 | tf_op jit(solution)/shard_map/ppermute | solution.py:57
  46.4 11.1 %collective-permute-done.11 = f32[192,128]{1,0:T(8,128)S(1)} collective-permute-done((f32[192,128]{1,0:T(8,128)S(1)}, f32[192,128]{1,0:T(8,128)S(1)}, u32[]{:S(2)}, u32[]{:S(2)}) %collective-permute-start.11) | collective-permute-done | bytes 98336 | tf_op jit(solution)/shard_map/ppermute | solution.py:57
  57.5 0.0 collective-permute-done.4
  57.6 0.2 add_bitcast_fusion
  57.8 1.1 %collective-permute-start.13 = (f32[256,256]{1,0:T(8,128)S(1)}, f32[256,256]{1,0:T(8,128)S(1)}, u32[]{:S(2)}, u32[]{:S(2)}) collective-permute-start(f32[256,256]{1,0:T(8,128)S(1)} %get-tuple-element.66), channel_id=1, source_target_pairs={{0,64},{1,17},{2,66},{3,19},{4,68},{5,21},{6,70},{7,23},{8,72},{9,... | collective-permute-start | bytes 786440 | tf_op jit(solution)/shard_map/ppermute | solution.py:44
  58.9 1.6 %collective-permute-start.14 = (f32[256,256]{1,0:T(8,128)S(1)}, f32[256,256]{1,0:T(8,128)S(1)}, u32[]{:S(2)}, u32[]{:S(2)}) collective-permute-start(f32[256,256]{1,0:T(8,128)S(1)} %get-tuple-element.65), channel_id=1, source_target_pairs={{0,32},{1,9},{2,34},{3,11},{4,36},{5,13},{6,38},{7,15},{8,40},{9,1... | collective-permute-start | bytes 786440 | tf_op jit(solution)/shard_map/ppermute | solution.py:44
  60.5 1.1 %collective-permute-start.15 = (f32[256,256]{1,0:T(8,128)S(1)}, f32[256,256]{1,0:T(8,128)S(1)}, u32[]{:S(2)}, u32[]{:S(2)}) collective-permute-start(f32[256,256]{1,0:T(8,128)S(1)} %get-tuple-element.64), channel_id=1, source_target_pairs={{0,96},{1,25},{2,98},{3,27},{4,100},{5,29},{6,102},{7,31},{8,104},... | collective-permute-start | bytes 786440 | tf_op jit(solution)/shard_map/ppermute | solution.py:44
  61.6 2.1 %collective-permute-start.12 = (f32[192,128]{1,0:T(8,128)S(1)}, f32[192,128]{1,0:T(8,128)S(1)}, u32[]{:S(2)}, u32[]{:S(2)}) collective-permute-start(f32[192,128]{1,0:T(8,128)S(1)} %add.101.mine), channel_id=1, source_target_pairs={{0,1},{1,0},{2,3},{3,2},{4,5},{5,4},{6,7},{7,6},{8,9},{9,8},{10,11... | collective-permute-start | bytes 294920 | tf_op jit(solution)/shard_map/ppermute | solution.py:48
  63.7 1.2 %collective-permute-done.13 = f32[256,256]{1,0:T(8,128)S(1)} collective-permute-done((f32[256,256]{1,0:T(8,128)S(1)}, f32[256,256]{1,0:T(8,128)S(1)}, u32[]{:S(2)}, u32[]{:S(2)}) %collective-permute-start.13) | collective-permute-done | bytes 262176 | tf_op jit(solution)/shard_map/ppermute | solution.py:44
  65.0 2.8 %collective-permute-done.14 = f32[256,256]{1,0:T(8,128)S(1)} collective-permute-done((f32[256,256]{1,0:T(8,128)S(1)}, f32[256,256]{1,0:T(8,128)S(1)}, u32[]{:S(2)}, u32[]{:S(2)}) %collective-permute-start.14) | collective-permute-done | bytes 262176 | tf_op jit(solution)/shard_map/ppermute | solution.py:44
  67.7 0.0 collective-permute-done.15
  67.7 0.1 fusion
  67.9 0.0 collective-permute-done.12.other
  67.9 1.7 %collective-permute-start.16 = (f32[256,256]{1,0:T(8,128)S(1)}, f32[256,256]{1,0:T(8,128)S(1)}, u32[]{:S(2)}, u32[]{:S(2)}) collective-permute-start(f32[256,256]{1,0:T(8,128)S(1)} %fusion), channel_id=1, source_target_pairs={{0,2},{1,3},{2,4},{3,5},{4,6},{5,7},{6,0},{7,1},{8,10},{9,11},{10,... | collective-permute-start | bytes 786440 | tf_op jit(solution)/shard_map/ppermute | solution.py:44
  69.6 3.3 %collective-permute-start.17 = (f32[256,256]{1,0:T(8,128)S(1)}, f32[256,256]{1,0:T(8,128)S(1)}, u32[]{:S(2)}, u32[]{:S(2)}) collective-permute-start(f32[256,256]{1,0:T(8,128)S(1)} %fusion), channel_id=1, source_target_pairs={{0,4},{1,5},{2,6},{3,7},{4,0},{5,1},{6,2},{7,3},{8,12},{9,13},{10,... | collective-permute-start | bytes 786440 | tf_op jit(solution)/shard_map/ppermute | solution.py:44
  72.9 0.7 collective-permute-start.18
  73.6 8.5 %inverse.1.refs_1_ = f32[256,256]{1,0:T(8,128)S(1)} custom-call(s32[5]{0:T(128)S(1)} %stack.23.place.refs_0_.refs_3_, f32[192,128]{1,0:T(8,128)S(1)} %add.101.mine, f32[192,128]{1,0:T(8,128)S(1)} %collective-permute-done.12.other), custom_call_target="tpu_custom_call" | custom-call | flops 8000000000 | bytes 4194304 | tf_op jit(solution)/shard_map/inverse/pallas_call | solution.py:266
  82.1 2.0 %convolution_multiply_fusion = f32[1024,256]{1,0:T(8,128)} fusion(f32[1024,256]{1,0:T(8,128)S(1)} %get-tuple-element.57, f32[256,256]{1,0:T(8,128)S(1)} %inverse.1.refs_1_), kind=kOutput, calls=%fused_computation | convolution fusion | flops 805568512 | bytes 2359296 | tf_op jit(solution)/shard_map/dot_general | solution.py:325
  84.1 0.0 collective-permute-done.16
  84.1 0.0 collective-permute-done.17
  84.1 0.0 collective-permute-done.18
  84.1 0.1 add_add_fusion.refs_2_
  84.1 1.8 %collective-permute-start.19 = (f32[256,256]{1,0:T(8,128)S(1)}, f32[256,256]{1,0:T(8,128)S(1)}, u32[]{:S(2)}, u32[]{:S(2)}) collective-permute-start(f32[256,256]{1,0:T(8,128)S(1)} %add_add_fusion.refs_2_), channel_id=1, source_target_pairs={{0,1},{1,0},{2,3},{3,2},{4,5},{5,4},{6,7},{7,6},{8,9},{9,8},{10,11... | collective-permute-start | bytes 786440 | tf_op jit(solution)/shard_map/ppermute | solution.py:48
  86.0 1.2 %collective-permute-done.19.refs_3_ = f32[256,256]{1,0:T(8,128)S(1)} collective-permute-done((f32[256,256]{1,0:T(8,128)S(1)}, f32[256,256]{1,0:T(8,128)S(1)}, u32[]{:S(2)}, u32[]{:S(2)}) %collective-permute-start.19) | collective-permute-done | bytes 262176 | tf_op jit(solution)/shard_map/ppermute | solution.py:48
  87.1 2.0 %finish.1 = f32[512,256]{1,0:T(8,128)} custom-call(s32[5]{0:T(128)S(1)} %stack.23.place.refs_0_.refs_3_, f32[256,256]{1,0:T(8,128)S(1)} %inverse.1.refs_1_, f32[256,256]{1,0:T(8,128)S(1)} %add_add_fusion.refs_2_, f32[256,256]{1,0:T(8,128)S(1)} %collective-permute-done.19.refs_3_), custom_call_target="tpu_custom_call" | custom-call | flops 402653184 | bytes 4194304 | tf_op jit(solution)/shard_map/finish/pallas_call | solution.py:266
  (11 shorter events, 0.1 us)
Async XLA Ops:
  11.4 4.5 %collective-permute-start = (f32[192,128]{1,0:T(8,128)S(1)}, f32[192,128]{1,0:T(8,128)S(1)}, u32[]{:S(2)}, u32[]{:S(2)}) collective-permute-start(f32[192,128]{1,0:T(8,128)S(1)} %get-tuple-element.34), channel_id=1, source_target_pairs={{0,1},{1,0},{2,3},{3,2},{4,5},{5,4},{6,7},{7,6},{8,9},{9,8},{10,11... | collective-permute-start | bytes 294920 | tf_op jit(solution)/shard_map/ppermute | solution.py:48
  15.8 8.4 %collective-permute-start.3 = (f32[8,256,256]{2,1,0:T(8,128)S(1)}, f32[8,256,256]{2,1,0:T(8,128)S(1)}, u32[]{:S(2)}, u32[]{:S(2)}) collective-permute-start(f32[8,256,256]{2,1,0:T(8,128)S(1)} %projection.5), channel_id=1, source_target_pairs={{0,1},{1,0},{2,3},{3,2},{4,5},{5,4},{6,7},{7,6},{8,9},{9,8},{10,11... | collective-permute-start | bytes 6291464 | tf_op jit(solution)/shard_map/ppermute | solution.py:48
  15.9 4.3 %collective-permute-start.1 = (f32[192,128]{1,0:T(8,128)S(1)}, f32[192,128]{1,0:T(8,128)S(1)}, u32[]{:S(2)}, u32[]{:S(2)}) collective-permute-start(f32[192,128]{1,0:T(8,128)S(1)} %add.95.refs_3_), channel_id=1, source_target_pairs={{0,8},{1,33},{2,10},{3,35},{4,12},{5,37},{6,14},{7,39},{8,0},{9,41... | collective-permute-start | bytes 294920 | tf_op jit(solution)/shard_map/ppermute | solution.py:57
  20.3 10.8 %collective-permute-start.6 = (f32[8,256,256]{2,1,0:T(8,128)S(1)}, f32[8,256,256]{2,1,0:T(8,128)S(1)}, u32[]{:S(2)}, u32[]{:S(2)}) collective-permute-start(f32[8,256,256]{2,1,0:T(8,128)S(1)} %projection.4), channel_id=1, source_target_pairs={{0,1},{1,0},{2,3},{3,2},{4,5},{5,4},{6,7},{7,6},{8,9},{9,8},{10,11... | collective-permute-start | bytes 6291464 | tf_op jit(solution)/shard_map/ppermute | solution.py:48
  21.1 6.0 %collective-permute-start.2 = (f32[192,128]{1,0:T(8,128)S(1)}, f32[192,128]{1,0:T(8,128)S(1)}, u32[]{:S(2)}, u32[]{:S(2)}) collective-permute-start(f32[192,128]{1,0:T(8,128)S(1)} %add.96.refs_3_), channel_id=1, source_target_pairs={{0,24},{1,97},{2,26},{3,99},{4,28},{5,101},{6,30},{7,103},{8,16},{... | collective-permute-start | bytes 294920 | tf_op jit(solution)/shard_map/ppermute | solution.py:57
  27.1 6.9 %collective-permute-start.5 = (f32[192,128]{1,0:T(8,128)S(1)}, f32[192,128]{1,0:T(8,128)S(1)}, u32[]{:S(2)}, u32[]{:S(2)}) collective-permute-start(f32[192,128]{1,0:T(8,128)S(1)} %add.97.refs_3_), channel_id=1, source_target_pairs={{0,32},{1,9},{2,34},{3,11},{4,36},{5,13},{6,38},{7,15},{8,40},{9,1... | collective-permute-start | bytes 294920 | tf_op jit(solution)/shard_map/ppermute | solution.py:57
  28.4 29.1 %collective-permute-start.4 = (f32[4,256,256]{2,1,0:T(8,128)S(1)}, f32[4,256,256]{2,1,0:T(8,128)S(1)}, u32[]{:S(2)}, u32[]{:S(2)}) collective-permute-start(f32[4,256,256]{2,1,0:T(8,128)S(1)} %get-tuple-element.43), channel_id=1, source_target_pairs={{0,8},{1,33},{2,10},{3,35},{4,12},{5,37},{6,14},{7,39},{8,16},{9,4... | collective-permute-start | bytes 3145736 | tf_op jit(solution)/shard_map/ppermute | solution.py:44
  28.4 29.1 %collective-permute-start.8 = (f32[4,256,256]{2,1,0:T(8,128)S(1)}, f32[4,256,256]{2,1,0:T(8,128)S(1)}, u32[]{:S(2)}, u32[]{:S(2)}) collective-permute-start(f32[4,256,256]{2,1,0:T(8,128)S(1)} %get-tuple-element.49), channel_id=1, source_target_pairs={{0,24},{1,97},{2,26},{3,99},{4,28},{5,101},{6,30},{7,103},{8,0},{9... | collective-permute-start | bytes 3145736 | tf_op jit(solution)/shard_map/ppermute | solution.py:44
  34.0 23.5 %collective-permute-start.7 = (f32[4,256,256]{2,1,0:T(8,128)S(1)}, f32[4,256,256]{2,1,0:T(8,128)S(1)}, u32[]{:S(2)}, u32[]{:S(2)}) collective-permute-start(f32[4,256,256]{2,1,0:T(8,128)S(1)} %get-tuple-element.48), channel_id=1, source_target_pairs={{0,16},{1,65},{2,18},{3,67},{4,20},{5,69},{6,22},{7,71},{8,24},{9,... | collective-permute-start | bytes 3145736 | tf_op jit(solution)/shard_map/ppermute | solution.py:44
  34.4 4.0 %collective-permute-start.9 = (f32[192,128]{1,0:T(8,128)S(1)}, f32[192,128]{1,0:T(8,128)S(1)}, u32[]{:S(2)}, u32[]{:S(2)}) collective-permute-start(f32[192,128]{1,0:T(8,128)S(1)} %add.98), channel_id=1, source_target_pairs={{0,2},{1,3},{2,0},{3,1},{4,6},{5,7},{6,4},{7,5},{8,10},{9,11},{10,... | collective-permute-start | bytes 294920 | tf_op jit(solution)/shard_map/ppermute | solution.py:57
  38.4 6.0 %collective-permute-start.10 = (f32[192,128]{1,0:T(8,128)S(1)}, f32[192,128]{1,0:T(8,128)S(1)}, u32[]{:S(2)}, u32[]{:S(2)}) collective-permute-start(f32[192,128]{1,0:T(8,128)S(1)} %add.99), channel_id=1, source_target_pairs={{0,6},{1,7},{2,4},{3,5},{4,2},{5,3},{6,0},{7,1},{8,14},{9,15},{10,... | collective-permute-start | bytes 294920 | tf_op jit(solution)/shard_map/ppermute | solution.py:57
  44.4 13.1 %collective-permute-start.11 = (f32[192,128]{1,0:T(8,128)S(1)}, f32[192,128]{1,0:T(8,128)S(1)}, u32[]{:S(2)}, u32[]{:S(2)}) collective-permute-start(f32[192,128]{1,0:T(8,128)S(1)} %add.100), channel_id=1, source_target_pairs={{0,96},{1,25},{2,98},{3,27},{4,100},{5,29},{6,102},{7,31},{8,104},... | collective-permute-start | bytes 294920 | tf_op jit(solution)/shard_map/ppermute | solution.py:57
  57.8 7.1 %collective-permute-start.13 = (f32[256,256]{1,0:T(8,128)S(1)}, f32[256,256]{1,0:T(8,128)S(1)}, u32[]{:S(2)}, u32[]{:S(2)}) collective-permute-start(f32[256,256]{1,0:T(8,128)S(1)} %get-tuple-element.66), channel_id=1, source_target_pairs={{0,64},{1,17},{2,66},{3,19},{4,68},{5,21},{6,70},{7,23},{8,72},{9,... | collective-permute-start | bytes 786440 | tf_op jit(solution)/shard_map/ppermute | solution.py:44
  58.9 8.8 %collective-permute-start.14 = (f32[256,256]{1,0:T(8,128)S(1)}, f32[256,256]{1,0:T(8,128)S(1)}, u32[]{:S(2)}, u32[]{:S(2)}) collective-permute-start(f32[256,256]{1,0:T(8,128)S(1)} %get-tuple-element.65), channel_id=1, source_target_pairs={{0,32},{1,9},{2,34},{3,11},{4,36},{5,13},{6,38},{7,15},{8,40},{9,1... | collective-permute-start | bytes 786440 | tf_op jit(solution)/shard_map/ppermute | solution.py:44
  60.5 7.2 %collective-permute-start.15 = (f32[256,256]{1,0:T(8,128)S(1)}, f32[256,256]{1,0:T(8,128)S(1)}, u32[]{:S(2)}, u32[]{:S(2)}) collective-permute-start(f32[256,256]{1,0:T(8,128)S(1)} %get-tuple-element.64), channel_id=1, source_target_pairs={{0,96},{1,25},{2,98},{3,27},{4,100},{5,29},{6,102},{7,31},{8,104},... | collective-permute-start | bytes 786440 | tf_op jit(solution)/shard_map/ppermute | solution.py:44
  61.6 6.3 %collective-permute-start.12 = (f32[192,128]{1,0:T(8,128)S(1)}, f32[192,128]{1,0:T(8,128)S(1)}, u32[]{:S(2)}, u32[]{:S(2)}) collective-permute-start(f32[192,128]{1,0:T(8,128)S(1)} %add.101.mine), channel_id=1, source_target_pairs={{0,1},{1,0},{2,3},{3,2},{4,5},{5,4},{6,7},{7,6},{8,9},{9,8},{10,11... | collective-permute-start | bytes 294920 | tf_op jit(solution)/shard_map/ppermute | solution.py:48
  67.9 16.2 %collective-permute-start.16 = (f32[256,256]{1,0:T(8,128)S(1)}, f32[256,256]{1,0:T(8,128)S(1)}, u32[]{:S(2)}, u32[]{:S(2)}) collective-permute-start(f32[256,256]{1,0:T(8,128)S(1)} %fusion), channel_id=1, source_target_pairs={{0,2},{1,3},{2,4},{3,5},{4,6},{5,7},{6,0},{7,1},{8,10},{9,11},{10,... | collective-permute-start | bytes 786440 | tf_op jit(solution)/shard_map/ppermute | solution.py:44
  69.6 14.5 %collective-permute-start.17 = (f32[256,256]{1,0:T(8,128)S(1)}, f32[256,256]{1,0:T(8,128)S(1)}, u32[]{:S(2)}, u32[]{:S(2)}) collective-permute-start(f32[256,256]{1,0:T(8,128)S(1)} %fusion), channel_id=1, source_target_pairs={{0,4},{1,5},{2,6},{3,7},{4,0},{5,1},{6,2},{7,3},{8,12},{9,13},{10,... | collective-permute-start | bytes 786440 | tf_op jit(solution)/shard_map/ppermute | solution.py:44
  72.9 11.2 %collective-permute-start.18 = (f32[256,256]{1,0:T(8,128)S(1)}, f32[256,256]{1,0:T(8,128)S(1)}, u32[]{:S(2)}, u32[]{:S(2)}) collective-permute-start(f32[256,256]{1,0:T(8,128)S(1)} %fusion), channel_id=1, source_target_pairs={{0,6},{1,7},{2,0},{3,1},{4,2},{5,3},{6,4},{7,5},{8,14},{9,15},{10,... | collective-permute-start | bytes 786440 | tf_op jit(solution)/shard_map/ppermute | solution.py:44
  84.1 3.0 %collective-permute-start.19 = (f32[256,256]{1,0:T(8,128)S(1)}, f32[256,256]{1,0:T(8,128)S(1)}, u32[]{:S(2)}, u32[]{:S(2)}) collective-permute-start(f32[256,256]{1,0:T(8,128)S(1)} %add_add_fusion.refs_2_), channel_id=1, source_target_pairs={{0,1},{1,0},{2,3},{3,2},{4,5},{5,4},{6,7},{7,6},{8,9},{9,8},{10,11... | collective-permute-start | bytes 786440 | tf_op jit(solution)/shard_map/ppermute | solution.py:48

commit v3 on v2

--- a/solution.py
+++ b/solution.py
@@ -293,8 +293,8 @@
 
     held, sketch, split, gram_mine, gram_other = sketch_call(place, row_counts, activations, sketch_matrix)
 
-    first = [(one, two) for one in (1, 3) for two in range(SIDE)]
-    second = [(one, two) for one in (2, 0) for two in range(SIDE)]
+    first = [(one, two) for one in (2, 0) for two in range(SIDE)]
+    second = [(one, two) for one in (1, 3) for two in range(SIDE)]
     first_far = swap_cores(projection_call(place, split, held, place, first, 1))
     packed = gram_mine + swap_cores(gram_other)
     second_far = projection_call(place, split, held, packed, second, 1)
@@ -303,10 +303,10 @@
     near = projection_call(place, split, held, packed, first, 0, first_far)
     packed, near = add_partner(packed, ("x", "y"), mirror, near)
     near, packed = lax.optimization_barrier((near, packed))
-    one, three = send(near[0], ("x", "y"), 1), send(near[1], ("x", "y"), 3)
+    two, mine = send(near[0], ("x", "y"), 2), near[1]
     near = projection_call(place, split, held, packed, second, 0, second_far)
-    packed, (to_two, mine) = add_partner(packed, ("y", "x"), flip, near)
-    two = send(to_two, ("x", "y"), 2)
+    packed, (to_one, to_three) = add_partner(packed, ("y", "x"), flip, near)
+    one, three = send(to_one, ("x", "y"), 1), send(to_three, ("x", "y"), 3)
     packed = add_partner(packed, ("z", "z"), flip)
     packed = add_partner(packed, ("z", "z"), mirror)
 
@@ -315,16 +315,16 @@
 
     one, two, three, packed = lax.optimization_barrier((one, two, three, packed))
     blocks = [(mine[j] + two[j]) + (one[j] + three[j]) for j in range(SIDE)]
-    arrived = [send(blocks[j], ("y", "x"), j) for j in range(1, SIDE)]
-    block = (blocks[0] + arrived[1]) + (arrived[0] + arrived[2])
+    two, three, one = (send(blocks[j], ("y", "x"), j) for j in (2, 3, 1))
+    block = (blocks[0] + two) + (one + three)
     packed, swapped, block = lax.optimization_barrier((packed, swapped, block))
-    arrived = [send(block, ("z", "z"), s) for s in range(1, SIDE)]
+    arrived = [send(block, ("z", "z"), s) for s in (2, 3, 1)]
     inverse = vmem_call(
         inverse_kernel, place, (packed, swapped), square, [pltpu.VMEM(square.shape, F32)], 8 * 10**9, "inverse"
     )
     basis = lax.dot_general(sketch, inverse, NT, precision=HIGH) * math.sqrt(total_rows)
     arrived, basis = lax.optimization_barrier((arrived, basis))
-    block = (block + arrived[1]) + (arrived[0] + arrived[2])
+    block = (block + arrived[0]) + (arrived[1] + arrived[2])
     projected = vmem_call(
         lambda *refs: finish_kernel(math.sqrt(width / total_rows), *refs), place,
         (inverse, block, swap_cores(block)), jax.ShapeDtypeStruct((2 * WIDE, columns), F32),

time: 89.2 us -> 88.6 us (level)
  waiting for transfers between devices: 20.9 us -> 18.7 us
  starting transfers between devices: 32 us -> 33.6 us
    ppermute x6, waiting for transfers between devices: 15.7 us -> 8.33 us  [add_partner(): arrived = lax.ppermute(value, BOTH, pairs(move))]
    ppermute x9, waiting for transfers between devices: 4.01 us -> 9.16 us  [send(): lax.ppermute(value, BOTH, pairs(lambda y, x, z, core: step_on(axes[core],...]
  transfers between devices with their start and end apart: 20 -> 20, of which waited for: 6 -> 8; matrix products, arithmetic and copies ran while one was open for 2% -> 3% of each run, Pallas kernels for 23% -> 23%
where the time goes in v3:
time: 88.6 us; the launch traced here: 88.5 us
  starting transfers between devices  33.6 us (38%)
  Pallas kernels  32.2 us (36%)
  waiting for transfers between devices  18.7 us (21%)
  matrix products  1.99 us (2%)
  between operations  1.41 us (2%)
    ppermute x6, starting transfers between devices, add_partner(): arrived = lax.ppermute(value, BOTH, pairs(move))  13.6 us
    ppermute x9, starting transfers between devices, send(): lax.ppermute(value, BOTH, pairs(lambda y, x, z, core: step_on(axes[core],...  13.3 us
    pallas_call x4, Pallas kernels, projection_call(): pl.pallas_call(lambda *refs: projection_kernel(offsets, other, *refs), ou...  11.7 us
    pallas_call x2, Pallas kernels, vmem_call(): pl.pallas_call(kernel, out_shape=out_shape, in_specs=[smem] + [vmem] * le...  10.5 us
    pallas_call x1, Pallas kernels, sketch_call(): pl.pallas_call(sketch_kernel, out_shape=[pltpu.VMEM((rows, width), BF16),...  10 us
    ppermute x9, waiting for transfers between devices, send(): lax.ppermute(value, BOTH, pairs(lambda y, x, z, core: step_on(axes[core],...  9.16 us
    ppermute x6, waiting for transfers between devices, add_partner(): arrived = lax.ppermute(value, BOTH, pairs(move))  8.33 us
    ppermute x5, starting transfers between devices, swap_cores(): lax.ppermute(value, BOTH, pairs(lambda y, x, z, core: (y, x, z, 1 - core)))  6.65 us
  transfers between devices with their start and end apart: 20, of which 8 were waited for; matrix products, arithmetic and copies ran while one was open for 3% of the time, Pallas kernels for 23%

profile of v3, /device:TPU:1, one launch (start us, length us, event | category | flops | bytes accessed | tf_op | source)
XLA Modules:
  0.0 88.5 jit_solution(7224144250257656518)
XLA Ops:
  1.3 0.1 stack.23.place.refs_0_.refs_3_
  1.4 10.0 %sketch.1 = (bf16[1024,8192]{1,0:T(8,128)(2,1)S(1)}, f32[1024,256]{1,0:T(8,128)S(1)}, bf16[512,1024]{1,0:T(8,128)(2,1)S(1)}, f32[192,128]{1,0:T(8,128)S(1)}, f32[192,128]{1,0:T(8,128)S(1)}) custom-call(s32[5]{0:T(128)S(1)} %stack.23.place.refs_0_.refs_3_, s32[1]{0:T(128)S(6)} %copy.5.count, bf16[1024,8192]{1,0:T(8,128)(2,1)} %act.1, bf16[8192,256]{1,0:T(8,128)(2,1)} %test.1), custom_call_target="tpu_custom_call" | custom-call | flops 4294967296 | bytes 20971520 | tf_op jit(solution)/shard_map/sketch/pallas_call | solution.py:126
  11.4 1.5 %collective-permute-start = (f32[192,128]{1,0:T(8,128)S(1)}, f32[192,128]{1,0:T(8,128)S(1)}, u32[]{:S(2)}, u32[]{:S(2)}) collective-permute-start(f32[192,128]{1,0:T(8,128)S(1)} %get-tuple-element.34), channel_id=1, source_target_pairs={{0,1},{1,0},{2,3},{3,2},{4,5},{5,4},{6,7},{7,6},{8,9},{9,8},{10,11... | collective-permute-start | bytes 294920 | tf_op jit(solution)/shard_map/ppermute | solution.py:48
  12.9 2.9 %projection.5 = f32[8,256,256]{2,1,0:T(8,128)S(1)} custom-call(s32[5]{0:T(128)S(1)} %stack.23.place.refs_0_.refs_3_, bf16[512,1024]{1,0:T(8,128)(2,1)S(1)} %get-tuple-element.35.refs_1_, bf16[1024,8192]{1,0:T(8,128)(2,1)S(1)} %get-tuple-element.36.refs_2_, s32[5]{0:T(128)S(1)} %stack.23.place.refs_0_.refs_3_), custom_call_target="tpu_custom_call" | custom-call | flops 2147483648 | bytes 4194304 | tf_op jit(solution)/shard_map/projection/pallas_call | solution.py:182
  15.8 0.1 collective-permute-start.3
  15.9 0.0 collective-permute-done
  15.9 1.4 %collective-permute-start.1 = (f32[192,128]{1,0:T(8,128)S(1)}, f32[192,128]{1,0:T(8,128)S(1)}, u32[]{:S(2)}, u32[]{:S(2)}) collective-permute-start(f32[192,128]{1,0:T(8,128)S(1)} %add.95.refs_3_), channel_id=1, source_target_pairs={{0,8},{1,33},{2,10},{3,35},{4,12},{5,37},{6,14},{7,39},{8,0},{9,41... | collective-permute-start | bytes 294920 | tf_op jit(solution)/shard_map/ppermute | solution.py:57
  17.4 2.9 %projection.4 = f32[8,256,256]{2,1,0:T(8,128)S(1)} custom-call(s32[5]{0:T(128)S(1)} %stack.23.place.refs_0_.refs_3_, bf16[512,1024]{1,0:T(8,128)(2,1)S(1)} %get-tuple-element.35.refs_1_, bf16[1024,8192]{1,0:T(8,128)(2,1)S(1)} %get-tuple-element.36.refs_2_, f32[192,128]{1,0:T(8,128)S(1)} %add.95.refs_3_), custom_call_target="tpu_custom_call" | custom-call | flops 2147483648 | bytes 4194304 | tf_op jit(solution)/shard_map/projection/pallas_call | solution.py:182
  20.3 0.0 collective-permute-done.1
  20.3 0.8 collective-permute-start.5
  21.1 3.0 %collective-permute-start.2 = (f32[192,128]{1,0:T(8,128)S(1)}, f32[192,128]{1,0:T(8,128)S(1)}, u32[]{:S(2)}, u32[]{:S(2)}) collective-permute-start(f32[192,128]{1,0:T(8,128)S(1)} %add.96.refs_3_), channel_id=1, source_target_pairs={{0,24},{1,97},{2,26},{3,99},{4,28},{5,101},{6,30},{7,103},{8,16},{... | collective-permute-start | bytes 294920 | tf_op jit(solution)/shard_map/ppermute | solution.py:57
  24.2 0.0 collective-permute-done.3.refs_4_
  24.2 2.9 %projection.6 = (f32[4,256,256]{2,1,0:T(8,128)S(1)}, f32[4,256,256]{2,1,0:T(8,128)S(1)}) custom-call(s32[5]{0:T(128)S(1)} %stack.23.place.refs_0_.refs_3_, bf16[512,1024]{1,0:T(8,128)(2,1)S(1)} %get-tuple-element.35.refs_1_, bf16[1024,8192]{1,0:T(8,128)(2,1)S(1)} %get-tuple-element.36.refs_2_, f32[192,128]{1,0:T(8,128)S(1)} %add.96.refs_3_, ...), custom_call_target="tpu_custom_call" | custom-call | flops 2147483648 | bytes 4194304 | tf_op jit(solution)/shard_map/projection/pallas_call | solution.py:182
  27.1 0.0 collective-permute-done.2
  27.1 1.3 %collective-permute-start.4 = (f32[192,128]{1,0:T(8,128)S(1)}, f32[192,128]{1,0:T(8,128)S(1)}, u32[]{:S(2)}, u32[]{:S(2)}) collective-permute-start(f32[192,128]{1,0:T(8,128)S(1)} %add.97.refs_3_), channel_id=1, source_target_pairs={{0,32},{1,9},{2,34},{3,11},{4,36},{5,13},{6,38},{7,15},{8,40},{9,1... | collective-permute-start | bytes 294920 | tf_op jit(solution)/shard_map/ppermute | solution.py:57
  28.4 1.0 %collective-permute-start.7 = (f32[4,256,256]{2,1,0:T(8,128)S(1)}, f32[4,256,256]{2,1,0:T(8,128)S(1)}, u32[]{:S(2)}, u32[]{:S(2)}) collective-permute-start(f32[4,256,256]{2,1,0:T(8,128)S(1)} %get-tuple-element.48), channel_id=1, source_target_pairs={{0,16},{1,65},{2,18},{3,67},{4,20},{5,69},{6,22},{7,71},{8,24},{9,... | collective-permute-start | bytes 3145736 | tf_op jit(solution)/shard_map/ppermute | solution.py:44
  29.4 2.9 %projection.7 = (f32[4,256,256]{2,1,0:T(8,128)S(1)}, f32[4,256,256]{2,1,0:T(8,128)S(1)}) custom-call(s32[5]{0:T(128)S(1)} %stack.23.place.refs_0_.refs_3_, bf16[512,1024]{1,0:T(8,128)(2,1)S(1)} %get-tuple-element.35.refs_1_, bf16[1024,8192]{1,0:T(8,128)(2,1)S(1)} %get-tuple-element.36.refs_2_, f32[192,128]{1,0:T(8,128)S(1)} %add.97.refs_3_, ...), custom_call_target="tpu_custom_call" | custom-call | flops 2147483648 | bytes 4194304 | tf_op jit(solution)/shard_map/projection/pallas_call | solution.py:182
  32.4 0.0 collective-permute-done.4
  32.4 1.4 %collective-permute-start.6 = (f32[4,256,256]{2,1,0:T(8,128)S(1)}, f32[4,256,256]{2,1,0:T(8,128)S(1)}, u32[]{:S(2)}, u32[]{:S(2)}) collective-permute-start(f32[4,256,256]{2,1,0:T(8,128)S(1)} %get-tuple-element.47), channel_id=1, source_target_pairs={{0,8},{1,33},{2,10},{3,35},{4,12},{5,37},{6,14},{7,39},{8,16},{9,4... | collective-permute-start | bytes 3145736 | tf_op jit(solution)/shard_map/ppermute | solution.py:44
  33.8 1.4 %collective-permute-start.8 = (f32[4,256,256]{2,1,0:T(8,128)S(1)}, f32[4,256,256]{2,1,0:T(8,128)S(1)}, u32[]{:S(2)}, u32[]{:S(2)}) collective-permute-start(f32[4,256,256]{2,1,0:T(8,128)S(1)} %get-tuple-element.49), channel_id=1, source_target_pairs={{0,24},{1,97},{2,26},{3,99},{4,28},{5,101},{6,30},{7,103},{8,0},{9... | collective-permute-start | bytes 3145736 | tf_op jit(solution)/shard_map/ppermute | solution.py:44
  35.1 1.7 %collective-permute-start.9 = (f32[192,128]{1,0:T(8,128)S(1)}, f32[192,128]{1,0:T(8,128)S(1)}, u32[]{:S(2)}, u32[]{:S(2)}) collective-permute-start(f32[192,128]{1,0:T(8,128)S(1)} %add.98), channel_id=1, source_target_pairs={{0,2},{1,3},{2,0},{3,1},{4,6},{5,7},{6,4},{7,5},{8,10},{9,11},{10,... | collective-permute-start | bytes 294920 | tf_op jit(solution)/shard_map/ppermute | solution.py:57
  36.9 2.3 %collective-permute-done.9 = f32[192,128]{1,0:T(8,128)S(1)} collective-permute-done((f32[192,128]{1,0:T(8,128)S(1)}, f32[192,128]{1,0:T(8,128)S(1)}, u32[]{:S(2)}, u32[]{:S(2)}) %collective-permute-start.9) | collective-permute-done | bytes 98336 | tf_op jit(solution)/shard_map/ppermute | solution.py:57
  39.2 3.7 %collective-permute-start.10 = (f32[192,128]{1,0:T(8,128)S(1)}, f32[192,128]{1,0:T(8,128)S(1)}, u32[]{:S(2)}, u32[]{:S(2)}) collective-permute-start(f32[192,128]{1,0:T(8,128)S(1)} %add.99), channel_id=1, source_target_pairs={{0,6},{1,7},{2,4},{3,5},{4,2},{5,3},{6,0},{7,1},{8,14},{9,15},{10,... | collective-permute-start | bytes 294920 | tf_op jit(solution)/shard_map/ppermute | solution.py:57
  42.9 2.3 %collective-permute-done.10 = f32[192,128]{1,0:T(8,128)S(1)} collective-permute-done((f32[192,128]{1,0:T(8,128)S(1)}, f32[192,128]{1,0:T(8,128)S(1)}, u32[]{:S(2)}, u32[]{:S(2)}) %collective-permute-start.10) | collective-permute-done | bytes 98336 | tf_op jit(solution)/shard_map/ppermute | solution.py:57
  45.2 2.5 %collective-permute-start.11 = (f32[192,128]{1,0:T(8,128)S(1)}, f32[192,128]{1,0:T(8,128)S(1)}, u32[]{:S(2)}, u32[]{:S(2)}) collective-permute-start(f32[192,128]{1,0:T(8,128)S(1)} %add.100), channel_id=1, source_target_pairs={{0,96},{1,25},{2,98},{3,27},{4,100},{5,29},{6,102},{7,31},{8,104},... | collective-permute-start | bytes 294920 | tf_op jit(solution)/shard_map/ppermute | solution.py:57
  47.7 3.7 %collective-permute-done.11 = f32[192,128]{1,0:T(8,128)S(1)} collective-permute-done((f32[192,128]{1,0:T(8,128)S(1)}, f32[192,128]{1,0:T(8,128)S(1)}, u32[]{:S(2)}, u32[]{:S(2)}) %collective-permute-start.11) | collective-permute-done | bytes 98336 | tf_op jit(solution)/shard_map/ppermute | solution.py:57
  51.4 5.7 %collective-permute-done.6 = f32[4,256,256]{2,1,0:T(8,128)S(1)} collective-permute-done((f32[4,256,256]{2,1,0:T(8,128)S(1)}, f32[4,256,256]{2,1,0:T(8,128)S(1)}, u32[]{:S(2)}, u32[]{:S(2)}) %collective-permute-start.6) | collective-permute-done | bytes 1048608 | tf_op jit(solution)/shard_map/ppermute | solution.py:44
  57.1 0.0 collective-permute-done.8
  57.1 0.2 add_bitcast_fusion
  57.4 1.8 %collective-permute-start.13 = (f32[256,256]{1,0:T(8,128)S(1)}, f32[256,256]{1,0:T(8,128)S(1)}, u32[]{:S(2)}, u32[]{:S(2)}) collective-permute-start(f32[256,256]{1,0:T(8,128)S(1)} %get-tuple-element.66), channel_id=1, source_target_pairs={{0,64},{1,17},{2,66},{3,19},{4,68},{5,21},{6,70},{7,23},{8,72},{9,... | collective-permute-start | bytes 786440 | tf_op jit(solution)/shard_map/ppermute | solution.py:44
  59.1 0.8 collective-permute-start.14
  60.0 1.8 %collective-permute-start.15 = (f32[256,256]{1,0:T(8,128)S(1)}, f32[256,256]{1,0:T(8,128)S(1)}, u32[]{:S(2)}, u32[]{:S(2)}) collective-permute-start(f32[256,256]{1,0:T(8,128)S(1)} %get-tuple-element.64), channel_id=1, source_target_pairs={{0,96},{1,25},{2,98},{3,27},{4,100},{5,29},{6,102},{7,31},{8,104},... | collective-permute-start | bytes 786440 | tf_op jit(solution)/shard_map/ppermute | solution.py:44
  61.8 2.2 %collective-permute-start.12 = (f32[192,128]{1,0:T(8,128)S(1)}, f32[192,128]{1,0:T(8,128)S(1)}, u32[]{:S(2)}, u32[]{:S(2)}) collective-permute-start(f32[192,128]{1,0:T(8,128)S(1)} %add.101.mine), channel_id=1, source_target_pairs={{0,1},{1,0},{2,3},{3,2},{4,5},{5,4},{6,7},{7,6},{8,9},{9,8},{10,11... | collective-permute-start | bytes 294920 | tf_op jit(solution)/shard_map/ppermute | solution.py:48
  64.0 0.5 collective-permute-done.13
  64.5 2.8 %collective-permute-done.14 = f32[256,256]{1,0:T(8,128)S(1)} collective-permute-done((f32[256,256]{1,0:T(8,128)S(1)}, f32[256,256]{1,0:T(8,128)S(1)}, u32[]{:S(2)}, u32[]{:S(2)}) %collective-permute-start.14) | collective-permute-done | bytes 262176 | tf_op jit(solution)/shard_map/ppermute | solution.py:44
  67.3 0.1 fusion
  67.4 0.0 collective-permute-done.12.other
  67.4 3.7 %collective-permute-start.16 = (f32[256,256]{1,0:T(8,128)S(1)}, f32[256,256]{1,0:T(8,128)S(1)}, u32[]{:S(2)}, u32[]{:S(2)}) collective-permute-start(f32[256,256]{1,0:T(8,128)S(1)} %fusion), channel_id=1, source_target_pairs={{0,4},{1,5},{2,6},{3,7},{4,0},{5,1},{6,2},{7,3},{8,12},{9,13},{10,... | collective-permute-start | bytes 786440 | tf_op jit(solution)/shard_map/ppermute | solution.py:44
  71.1 0.5 collective-permute-start.17
  71.6 1.0 %collective-permute-start.18 = (f32[256,256]{1,0:T(8,128)S(1)}, f32[256,256]{1,0:T(8,128)S(1)}, u32[]{:S(2)}, u32[]{:S(2)}) collective-permute-start(f32[256,256]{1,0:T(8,128)S(1)} %fusion), channel_id=1, source_target_pairs={{0,2},{1,3},{2,4},{3,5},{4,6},{5,7},{6,0},{7,1},{8,10},{9,11},{10,... | collective-permute-start | bytes 786440 | tf_op jit(solution)/shard_map/ppermute | solution.py:44
  72.6 8.5 %inverse.1.refs_1_ = f32[256,256]{1,0:T(8,128)S(1)} custom-call(s32[5]{0:T(128)S(1)} %stack.23.place.refs_0_.refs_3_, f32[192,128]{1,0:T(8,128)S(1)} %add.101.mine, f32[192,128]{1,0:T(8,128)S(1)} %collective-permute-done.12.other), custom_call_target="tpu_custom_call" | custom-call | flops 8000000000 | bytes 4194304 | tf_op jit(solution)/shard_map/inverse/pallas_call | solution.py:266
  81.1 2.0 %convolution_multiply_fusion = f32[1024,256]{1,0:T(8,128)} fusion(f32[1024,256]{1,0:T(8,128)S(1)} %get-tuple-element.57, f32[256,256]{1,0:T(8,128)S(1)} %inverse.1.refs_1_), kind=kOutput, calls=%fused_computation | convolution fusion | flops 805568512 | bytes 2359296 | tf_op jit(solution)/shard_map/dot_general | solution.py:325
  83.1 0.0 collective-permute-done.16
  83.1 0.1 collective-permute-done.17
  83.2 0.1 add_add_fusion.refs_2_
  83.3 2.0 %collective-permute-start.19 = (f32[256,256]{1,0:T(8,128)S(1)}, f32[256,256]{1,0:T(8,128)S(1)}, u32[]{:S(2)}, u32[]{:S(2)}) collective-permute-start(f32[256,256]{1,0:T(8,128)S(1)} %add_add_fusion.refs_2_), channel_id=1, source_target_pairs={{0,1},{1,0},{2,3},{3,2},{4,5},{5,4},{6,7},{7,6},{8,9},{9,8},{10,11... | collective-permute-start | bytes 786440 | tf_op jit(solution)/shard_map/ppermute | solution.py:48
  85.3 1.2 %collective-permute-done.19.refs_3_ = f32[256,256]{1,0:T(8,128)S(1)} collective-permute-done((f32[256,256]{1,0:T(8,128)S(1)}, f32[256,256]{1,0:T(8,128)S(1)}, u32[]{:S(2)}, u32[]{:S(2)}) %collective-permute-start.19) | collective-permute-done | bytes 262176 | tf_op jit(solution)/shard_map/ppermute | solution.py:48
  86.5 2.0 %finish.1 = f32[512,256]{1,0:T(8,128)} custom-call(s32[5]{0:T(128)S(1)} %stack.23.place.refs_0_.refs_3_, f32[256,256]{1,0:T(8,128)S(1)} %inverse.1.refs_1_, f32[256,256]{1,0:T(8,128)S(1)} %add_add_fusion.refs_2_, f32[256,256]{1,0:T(8,128)S(1)} %collective-permute-done.19.refs_3_), custom_call_target="tpu_custom_call" | custom-call | flops 402653184 | bytes 4194304 | tf_op jit(solution)/shard_map/finish/pallas_call | solution.py:266
  (11 shorter events, 0.1 us)
Async XLA Ops:
  11.4 4.5 %collective-permute-start = (f32[192,128]{1,0:T(8,128)S(1)}, f32[192,128]{1,0:T(8,128)S(1)}, u32[]{:S(2)}, u32[]{:S(2)}) collective-permute-start(f32[192,128]{1,0:T(8,128)S(1)} %get-tuple-element.34), channel_id=1, source_target_pairs={{0,1},{1,0},{2,3},{3,2},{4,5},{5,4},{6,7},{7,6},{8,9},{9,8},{10,11... | collective-permute-start | bytes 294920 | tf_op jit(solution)/shard_map/ppermute | solution.py:48
  15.8 8.4 %collective-permute-start.3 = (f32[8,256,256]{2,1,0:T(8,128)S(1)}, f32[8,256,256]{2,1,0:T(8,128)S(1)}, u32[]{:S(2)}, u32[]{:S(2)}) collective-permute-start(f32[8,256,256]{2,1,0:T(8,128)S(1)} %projection.5), channel_id=1, source_target_pairs={{0,1},{1,0},{2,3},{3,2},{4,5},{5,4},{6,7},{7,6},{8,9},{9,8},{10,11... | collective-permute-start | bytes 6291464 | tf_op jit(solution)/shard_map/ppermute | solution.py:48
  15.9 4.3 %collective-permute-start.1 = (f32[192,128]{1,0:T(8,128)S(1)}, f32[192,128]{1,0:T(8,128)S(1)}, u32[]{:S(2)}, u32[]{:S(2)}) collective-permute-start(f32[192,128]{1,0:T(8,128)S(1)} %add.95.refs_3_), channel_id=1, source_target_pairs={{0,8},{1,33},{2,10},{3,35},{4,12},{5,37},{6,14},{7,39},{8,0},{9,41... | collective-permute-start | bytes 294920 | tf_op jit(solution)/shard_map/ppermute | solution.py:57
  20.3 9.1 %collective-permute-start.5 = (f32[8,256,256]{2,1,0:T(8,128)S(1)}, f32[8,256,256]{2,1,0:T(8,128)S(1)}, u32[]{:S(2)}, u32[]{:S(2)}) collective-permute-start(f32[8,256,256]{2,1,0:T(8,128)S(1)} %projection.4), channel_id=1, source_target_pairs={{0,1},{1,0},{2,3},{3,2},{4,5},{5,4},{6,7},{7,6},{8,9},{9,8},{10,11... | collective-permute-start | bytes 6291464 | tf_op jit(solution)/shard_map/ppermute | solution.py:48
  21.1 6.0 %collective-permute-start.2 = (f32[192,128]{1,0:T(8,128)S(1)}, f32[192,128]{1,0:T(8,128)S(1)}, u32[]{:S(2)}, u32[]{:S(2)}) collective-permute-start(f32[192,128]{1,0:T(8,128)S(1)} %add.96.refs_3_), channel_id=1, source_target_pairs={{0,24},{1,97},{2,26},{3,99},{4,28},{5,101},{6,30},{7,103},{8,16},{... | collective-permute-start | bytes 294920 | tf_op jit(solution)/shard_map/ppermute | solution.py:57
  27.1 5.2 %collective-permute-start.4 = (f32[192,128]{1,0:T(8,128)S(1)}, f32[192,128]{1,0:T(8,128)S(1)}, u32[]{:S(2)}, u32[]{:S(2)}) collective-permute-start(f32[192,128]{1,0:T(8,128)S(1)} %add.97.refs_3_), channel_id=1, source_target_pairs={{0,32},{1,9},{2,34},{3,11},{4,36},{5,13},{6,38},{7,15},{8,40},{9,1... | collective-permute-start | bytes 294920 | tf_op jit(solution)/shard_map/ppermute | solution.py:57
  28.4 22.9 %collective-permute-start.7 = (f32[4,256,256]{2,1,0:T(8,128)S(1)}, f32[4,256,256]{2,1,0:T(8,128)S(1)}, u32[]{:S(2)}, u32[]{:S(2)}) collective-permute-start(f32[4,256,256]{2,1,0:T(8,128)S(1)} %get-tuple-element.48), channel_id=1, source_target_pairs={{0,16},{1,65},{2,18},{3,67},{4,20},{5,69},{6,22},{7,71},{8,24},{9,... | collective-permute-start | bytes 3145736 | tf_op jit(solution)/shard_map/ppermute | solution.py:44
  32.4 24.7 %collective-permute-start.6 = (f32[4,256,256]{2,1,0:T(8,128)S(1)}, f32[4,256,256]{2,1,0:T(8,128)S(1)}, u32[]{:S(2)}, u32[]{:S(2)}) collective-permute-start(f32[4,256,256]{2,1,0:T(8,128)S(1)} %get-tuple-element.47), channel_id=1, source_target_pairs={{0,8},{1,33},{2,10},{3,35},{4,12},{5,37},{6,14},{7,39},{8,16},{9,4... | collective-permute-start | bytes 3145736 | tf_op jit(solution)/shard_map/ppermute | solution.py:44
  33.8 23.4 %collective-permute-start.8 = (f32[4,256,256]{2,1,0:T(8,128)S(1)}, f32[4,256,256]{2,1,0:T(8,128)S(1)}, u32[]{:S(2)}, u32[]{:S(2)}) collective-permute-start(f32[4,256,256]{2,1,0:T(8,128)S(1)} %get-tuple-element.49), channel_id=1, source_target_pairs={{0,24},{1,97},{2,26},{3,99},{4,28},{5,101},{6,30},{7,103},{8,0},{9... | collective-permute-start | bytes 3145736 | tf_op jit(solution)/shard_map/ppermute | solution.py:44
  35.1 4.0 %collective-permute-start.9 = (f32[192,128]{1,0:T(8,128)S(1)}, f32[192,128]{1,0:T(8,128)S(1)}, u32[]{:S(2)}, u32[]{:S(2)}) collective-permute-start(f32[192,128]{1,0:T(8,128)S(1)} %add.98), channel_id=1, source_target_pairs={{0,2},{1,3},{2,0},{3,1},{4,6},{5,7},{6,4},{7,5},{8,10},{9,11},{10,... | collective-permute-start | bytes 294920 | tf_op jit(solution)/shard_map/ppermute | solution.py:57
  39.2 6.0 %collective-permute-start.10 = (f32[192,128]{1,0:T(8,128)S(1)}, f32[192,128]{1,0:T(8,128)S(1)}, u32[]{:S(2)}, u32[]{:S(2)}) collective-permute-start(f32[192,128]{1,0:T(8,128)S(1)} %add.99), channel_id=1, source_target_pairs={{0,6},{1,7},{2,4},{3,5},{4,2},{5,3},{6,0},{7,1},{8,14},{9,15},{10,... | collective-permute-start | bytes 294920 | tf_op jit(solution)/shard_map/ppermute | solution.py:57
  45.2 6.2 %collective-permute-start.11 = (f32[192,128]{1,0:T(8,128)S(1)}, f32[192,128]{1,0:T(8,128)S(1)}, u32[]{:S(2)}, u32[]{:S(2)}) collective-permute-start(f32[192,128]{1,0:T(8,128)S(1)} %add.100), channel_id=1, source_target_pairs={{0,96},{1,25},{2,98},{3,27},{4,100},{5,29},{6,102},{7,31},{8,104},... | collective-permute-start | bytes 294920 | tf_op jit(solution)/shard_map/ppermute | solution.py:57
  57.4 7.1 %collective-permute-start.13 = (f32[256,256]{1,0:T(8,128)S(1)}, f32[256,256]{1,0:T(8,128)S(1)}, u32[]{:S(2)}, u32[]{:S(2)}) collective-permute-start(f32[256,256]{1,0:T(8,128)S(1)} %get-tuple-element.66), channel_id=1, source_target_pairs={{0,64},{1,17},{2,66},{3,19},{4,68},{5,21},{6,70},{7,23},{8,72},{9,... | collective-permute-start | bytes 786440 | tf_op jit(solution)/shard_map/ppermute | solution.py:44
  59.1 8.1 %collective-permute-start.14 = (f32[256,256]{1,0:T(8,128)S(1)}, f32[256,256]{1,0:T(8,128)S(1)}, u32[]{:S(2)}, u32[]{:S(2)}) collective-permute-start(f32[256,256]{1,0:T(8,128)S(1)} %get-tuple-element.65), channel_id=1, source_target_pairs={{0,32},{1,9},{2,34},{3,11},{4,36},{5,13},{6,38},{7,15},{8,40},{9,1... | collective-permute-start | bytes 786440 | tf_op jit(solution)/shard_map/ppermute | solution.py:44
  60.0 7.3 %collective-permute-start.15 = (f32[256,256]{1,0:T(8,128)S(1)}, f32[256,256]{1,0:T(8,128)S(1)}, u32[]{:S(2)}, u32[]{:S(2)}) collective-permute-start(f32[256,256]{1,0:T(8,128)S(1)} %get-tuple-element.64), channel_id=1, source_target_pairs={{0,96},{1,25},{2,98},{3,27},{4,100},{5,29},{6,102},{7,31},{8,104},... | collective-permute-start | bytes 786440 | tf_op jit(solution)/shard_map/ppermute | solution.py:44
  61.8 5.6 %collective-permute-start.12 = (f32[192,128]{1,0:T(8,128)S(1)}, f32[192,128]{1,0:T(8,128)S(1)}, u32[]{:S(2)}, u32[]{:S(2)}) collective-permute-start(f32[192,128]{1,0:T(8,128)S(1)} %add.101.mine), channel_id=1, source_target_pairs={{0,1},{1,0},{2,3},{3,2},{4,5},{5,4},{6,7},{7,6},{8,9},{9,8},{10,11... | collective-permute-start | bytes 294920 | tf_op jit(solution)/shard_map/ppermute | solution.py:48
  67.4 15.6 %collective-permute-start.16 = (f32[256,256]{1,0:T(8,128)S(1)}, f32[256,256]{1,0:T(8,128)S(1)}, u32[]{:S(2)}, u32[]{:S(2)}) collective-permute-start(f32[256,256]{1,0:T(8,128)S(1)} %fusion), channel_id=1, source_target_pairs={{0,4},{1,5},{2,6},{3,7},{4,0},{5,1},{6,2},{7,3},{8,12},{9,13},{10,... | collective-permute-start | bytes 786440 | tf_op jit(solution)/shard_map/ppermute | solution.py:44
  71.1 12.1 %collective-permute-start.17 = (f32[256,256]{1,0:T(8,128)S(1)}, f32[256,256]{1,0:T(8,128)S(1)}, u32[]{:S(2)}, u32[]{:S(2)}) collective-permute-start(f32[256,256]{1,0:T(8,128)S(1)} %fusion), channel_id=1, source_target_pairs={{0,6},{1,7},{2,0},{3,1},{4,2},{5,3},{6,4},{7,5},{8,14},{9,15},{10,... | collective-permute-start | bytes 786440 | tf_op jit(solution)/shard_map/ppermute | solution.py:44
  71.6 11.6 %collective-permute-start.18 = (f32[256,256]{1,0:T(8,128)S(1)}, f32[256,256]{1,0:T(8,128)S(1)}, u32[]{:S(2)}, u32[]{:S(2)}) collective-permute-start(f32[256,256]{1,0:T(8,128)S(1)} %fusion), channel_id=1, source_target_pairs={{0,2},{1,3},{2,4},{3,5},{4,6},{5,7},{6,0},{7,1},{8,10},{9,11},{10,... | collective-permute-start | bytes 786440 | tf_op jit(solution)/shard_map/ppermute | solution.py:44
  83.3 3.2 %collective-permute-start.19 = (f32[256,256]{1,0:T(8,128)S(1)}, f32[256,256]{1,0:T(8,128)S(1)}, u32[]{:S(2)}, u32[]{:S(2)}) collective-permute-start(f32[256,256]{1,0:T(8,128)S(1)} %add_add_fusion.refs_2_), channel_id=1, source_target_pairs={{0,1},{1,0},{2,3},{3,2},{4,5},{5,4},{6,7},{7,6},{8,9},{9,8},{10,11... | collective-permute-start | bytes 786440 | tf_op jit(solution)/shard_map/ppermute | solution.py:48

commit v4 on v3

--- a/solution.py
+++ b/solution.py
@@ -275,12 +275,18 @@
     )(place, *operands)
 
 
-def finish_kernel(scale, place, inverse, mine, other, projected):
-    wide = mine.shape[1]
+def finish_kernel(scale, place, inverse, block, mine, projected):
+    wide = block.shape[1]
     core = place[4]
-    for source, side in ((mine, core), (other, 1 - core)):
-        rows = lax.dot_general(source[...].T, inverse[...], NT, precision=HIGH, preferred_element_type=F32)
-        projected[pl.ds(pl.multiple_of(side * wide, wide), wide), :] = rows * scale
+    rows = lax.dot_general(block[...].T, inverse[...], NT, precision=HIGH, preferred_element_type=F32)
+    projected[pl.ds(pl.multiple_of(core * wide, wide), wide), :] = mine[...]
+    projected[pl.ds(pl.multiple_of((1 - core) * wide, wide), wide), :] = rows * scale
+
+
+def finish_mine(scale, place, inverse, block, rows):
+    rows[...] = scale * lax.dot_general(
+        block[...].T, inverse[...], NT, precision=HIGH, preferred_element_type=F32
+    )
 
 
 def on_device(activations, sketch_matrix, row_counts):
@@ -325,10 +331,15 @@
     basis = lax.dot_general(sketch, inverse, NT, precision=HIGH) * math.sqrt(total_rows)
     arrived, basis = lax.optimization_barrier((arrived, basis))
     block = (block + arrived[0]) + (arrived[1] + arrived[2])
+    scale = math.sqrt(width / total_rows)
+    other = swap_cores(block)
+    rows = vmem_call(
+        lambda *refs: finish_mine(scale, *refs), place, (inverse, block), square, [], 10**9, "finish_mine"
+    )
+    other, rows = lax.optimization_barrier((other, rows))
     projected = vmem_call(
-        lambda *refs: finish_kernel(math.sqrt(width / total_rows), *refs), place,
-        (inverse, block, swap_cores(block)), jax.ShapeDtypeStruct((2 * WIDE, columns), F32),
-        [], 24 * columns**2 * WIDE, "finish",
+        lambda *refs: finish_kernel(scale, *refs), place, (inverse, other, rows),
+        jax.ShapeDtypeStruct((2 * WIDE, columns), F32), [], 10**9, "finish",
     )
     return (basis, projected)
 

time: 88.6 us -> 88.4 us (level)
  waiting for transfers between devices: 18.7 us -> 17.7 us
    ppermute x5, waiting for transfers between devices: 1.17 us -> 0.2 us  [swap_cores(): lax.ppermute(value, BOTH, pairs(lambda y, x, z, core: (y, x, z, 1 - core)))]
    pallas_call x2 -> x3, Pallas kernels: 10.5 us -> 11.2 us  [vmem_call(): pl.pallas_call(kernel, out_shape=out_shape, in_specs=[smem] + [vmem] * le...]
  transfers between devices with their start and end apart: 20 -> 20, of which waited for: 8 -> 8; matrix products, arithmetic and copies ran while one was open for 3% -> 3% of each run, Pallas kernels for 23% -> 24%
where the time goes in v4:
time: 88.4 us; the launch traced here: 88.2 us
  starting transfers between devices  33.6 us (38%)
  Pallas kernels  32.9 us (37%)
  waiting for transfers between devices  17.7 us (20%)
  matrix products  1.99 us (2%)
  between operations  1.42 us (2%)
    ppermute x6, starting transfers between devices, add_partner(): arrived = lax.ppermute(value, BOTH, pairs(move))  13.6 us
    ppermute x9, starting transfers between devices, send(): lax.ppermute(value, BOTH, pairs(lambda y, x, z, core: step_on(axes[core],...  13.3 us
    pallas_call x4, Pallas kernels, projection_call(): pl.pallas_call(lambda *refs: projection_kernel(offsets, other, *refs), ou...  11.7 us
    pallas_call x3, Pallas kernels, vmem_call(): pl.pallas_call(kernel, out_shape=out_shape, in_specs=[smem] + [vmem] * le...  11.2 us
    pallas_call x1, Pallas kernels, sketch_call(): pl.pallas_call(sketch_kernel, out_shape=[pltpu.VMEM((rows, width), BF16),...  10 us
    ppermute x9, waiting for transfers between devices, send(): lax.ppermute(value, BOTH, pairs(lambda y, x, z, core: step_on(axes[core],...  9.16 us
    ppermute x6, waiting for transfers between devices, add_partner(): arrived = lax.ppermute(value, BOTH, pairs(move))  8.33 us
    ppermute x5, starting transfers between devices, swap_cores(): lax.ppermute(value, BOTH, pairs(lambda y, x, z, core: (y, x, z, 1 - core)))  6.65 us
  transfers between devices with their start and end apart: 20, of which 8 were waited for; matrix products, arithmetic and copies ran while one was open for 3% of the time, Pallas kernels for 24%

profile of v4, /device:TPU:1, one launch (start us, length us, event | category | flops | bytes accessed | tf_op | source)
XLA Modules:
  0.0 88.2 jit_solution(6046251909619798718)
XLA Ops:
  1.3 0.1 stack.23.place.refs_0_.refs_3_
  1.4 10.0 %sketch.1 = (bf16[1024,8192]{1,0:T(8,128)(2,1)S(1)}, f32[1024,256]{1,0:T(8,128)S(1)}, bf16[512,1024]{1,0:T(8,128)(2,1)S(1)}, f32[192,128]{1,0:T(8,128)S(1)}, f32[192,128]{1,0:T(8,128)S(1)}) custom-call(s32[5]{0:T(128)S(1)} %stack.23.place.refs_0_.refs_3_, s32[1]{0:T(128)S(6)} %copy.5.count, bf16[1024,8192]{1,0:T(8,128)(2,1)} %act.1, bf16[8192,256]{1,0:T(8,128)(2,1)} %test.1), custom_call_target="tpu_custom_call" | custom-call | flops 4294967296 | bytes 20971520 | tf_op jit(solution)/shard_map/sketch/pallas_call | solution.py:126
  11.4 1.5 %collective-permute-start = (f32[192,128]{1,0:T(8,128)S(1)}, f32[192,128]{1,0:T(8,128)S(1)}, u32[]{:S(2)}, u32[]{:S(2)}) collective-permute-start(f32[192,128]{1,0:T(8,128)S(1)} %get-tuple-element.36), channel_id=1, source_target_pairs={{0,1},{1,0},{2,3},{3,2},{4,5},{5,4},{6,7},{7,6},{8,9},{9,8},{10,11... | collective-permute-start | bytes 294920 | tf_op jit(solution)/shard_map/ppermute | solution.py:48
  12.9 2.9 %projection.5 = f32[8,256,256]{2,1,0:T(8,128)S(1)} custom-call(s32[5]{0:T(128)S(1)} %stack.23.place.refs_0_.refs_3_, bf16[512,1024]{1,0:T(8,128)(2,1)S(1)} %get-tuple-element.37.refs_1_, bf16[1024,8192]{1,0:T(8,128)(2,1)S(1)} %get-tuple-element.38.refs_2_, s32[5]{0:T(128)S(1)} %stack.23.place.refs_0_.refs_3_), custom_call_target="tpu_custom_call" | custom-call | flops 2147483648 | bytes 4194304 | tf_op jit(solution)/shard_map/projection/pallas_call | solution.py:182
  15.8 0.1 collective-permute-start.3
  15.9 0.0 collective-permute-done
  15.9 1.4 %collective-permute-start.1 = (f32[192,128]{1,0:T(8,128)S(1)}, f32[192,128]{1,0:T(8,128)S(1)}, u32[]{:S(2)}, u32[]{:S(2)}) collective-permute-start(f32[192,128]{1,0:T(8,128)S(1)} %add.95.refs_3_), channel_id=1, source_target_pairs={{0,8},{1,33},{2,10},{3,35},{4,12},{5,37},{6,14},{7,39},{8,0},{9,41... | collective-permute-start | bytes 294920 | tf_op jit(solution)/shard_map/ppermute | solution.py:57
  17.4 2.9 %projection.4 = f32[8,256,256]{2,1,0:T(8,128)S(1)} custom-call(s32[5]{0:T(128)S(1)} %stack.23.place.refs_0_.refs_3_, bf16[512,1024]{1,0:T(8,128)(2,1)S(1)} %get-tuple-element.37.refs_1_, bf16[1024,8192]{1,0:T(8,128)(2,1)S(1)} %get-tuple-element.38.refs_2_, f32[192,128]{1,0:T(8,128)S(1)} %add.95.refs_3_), custom_call_target="tpu_custom_call" | custom-call | flops 2147483648 | bytes 4194304 | tf_op jit(solution)/shard_map/projection/pallas_call | solution.py:182
  20.3 0.8 collective-permute-start.5
  21.1 3.0 %collective-permute-start.2 = (f32[192,128]{1,0:T(8,128)S(1)}, f32[192,128]{1,0:T(8,128)S(1)}, u32[]{:S(2)}, u32[]{:S(2)}) collective-permute-start(f32[192,128]{1,0:T(8,128)S(1)} %add.96.refs_3_), channel_id=1, source_target_pairs={{0,24},{1,97},{2,26},{3,99},{4,28},{5,101},{6,30},{7,103},{8,16},{... | collective-permute-start | bytes 294920 | tf_op jit(solution)/shard_map/ppermute | solution.py:57
  24.2 0.0 collective-permute-done.3.refs_4_
  24.2 2.9 %projection.6 = (f32[4,256,256]{2,1,0:T(8,128)S(1)}, f32[4,256,256]{2,1,0:T(8,128)S(1)}) custom-call(s32[5]{0:T(128)S(1)} %stack.23.place.refs_0_.refs_3_, bf16[512,1024]{1,0:T(8,128)(2,1)S(1)} %get-tuple-element.37.refs_1_, bf16[1024,8192]{1,0:T(8,128)(2,1)S(1)} %get-tuple-element.38.refs_2_, f32[192,128]{1,0:T(8,128)S(1)} %add.96.refs_3_, ...), custom_call_target="tpu_custom_call" | custom-call | flops 2147483648 | bytes 4194304 | tf_op jit(solution)/shard_map/projection/pallas_call | solution.py:182
  27.1 0.0 collective-permute-done.2
  27.1 1.3 %collective-permute-start.4 = (f32[192,128]{1,0:T(8,128)S(1)}, f32[192,128]{1,0:T(8,128)S(1)}, u32[]{:S(2)}, u32[]{:S(2)}) collective-permute-start(f32[192,128]{1,0:T(8,128)S(1)} %add.97.refs_3_), channel_id=1, source_target_pairs={{0,32},{1,9},{2,34},{3,11},{4,36},{5,13},{6,38},{7,15},{8,40},{9,1... | collective-permute-start | bytes 294920 | tf_op jit(solution)/shard_map/ppermute | solution.py:57
  28.4 1.0 %collective-permute-start.7 = (f32[4,256,256]{2,1,0:T(8,128)S(1)}, f32[4,256,256]{2,1,0:T(8,128)S(1)}, u32[]{:S(2)}, u32[]{:S(2)}) collective-permute-start(f32[4,256,256]{2,1,0:T(8,128)S(1)} %get-tuple-element.50), channel_id=1, source_target_pairs={{0,16},{1,65},{2,18},{3,67},{4,20},{5,69},{6,22},{7,71},{8,24},{9,... | collective-permute-start | bytes 3145736 | tf_op jit(solution)/shard_map/ppermute | solution.py:44
  29.4 2.9 %projection.7 = (f32[4,256,256]{2,1,0:T(8,128)S(1)}, f32[4,256,256]{2,1,0:T(8,128)S(1)}) custom-call(s32[5]{0:T(128)S(1)} %stack.23.place.refs_0_.refs_3_, bf16[512,1024]{1,0:T(8,128)(2,1)S(1)} %get-tuple-element.37.refs_1_, bf16[1024,8192]{1,0:T(8,128)(2,1)S(1)} %get-tuple-element.38.refs_2_, f32[192,128]{1,0:T(8,128)S(1)} %add.97.refs_3_, ...), custom_call_target="tpu_custom_call" | custom-call | flops 2147483648 | bytes 4194304 | tf_op jit(solution)/shard_map/projection/pallas_call | solution.py:182
  32.4 0.0 collective-permute-done.4
  32.4 1.4 %collective-permute-start.6 = (f32[4,256,256]{2,1,0:T(8,128)S(1)}, f32[4,256,256]{2,1,0:T(8,128)S(1)}, u32[]{:S(2)}, u32[]{:S(2)}) collective-permute-start(f32[4,256,256]{2,1,0:T(8,128)S(1)} %get-tuple-element.49), channel_id=1, source_target_pairs={{0,8},{1,33},{2,10},{3,35},{4,12},{5,37},{6,14},{7,39},{8,16},{9,4... | collective-permute-start | bytes 3145736 | tf_op jit(solution)/shard_map/ppermute | solution.py:44
  33.8 1.4 %collective-permute-start.8 = (f32[4,256,256]{2,1,0:T(8,128)S(1)}, f32[4,256,256]{2,1,0:T(8,128)S(1)}, u32[]{:S(2)}, u32[]{:S(2)}) collective-permute-start(f32[4,256,256]{2,1,0:T(8,128)S(1)} %get-tuple-element.51), channel_id=1, source_target_pairs={{0,24},{1,97},{2,26},{3,99},{4,28},{5,101},{6,30},{7,103},{8,0},{9... | collective-permute-start | bytes 3145736 | tf_op jit(solution)/shard_map/ppermute | solution.py:44
  35.1 1.7 %collective-permute-start.9 = (f32[192,128]{1,0:T(8,128)S(1)}, f32[192,128]{1,0:T(8,128)S(1)}, u32[]{:S(2)}, u32[]{:S(2)}) collective-permute-start(f32[192,128]{1,0:T(8,128)S(1)} %add.98), channel_id=1, source_target_pairs={{0,2},{1,3},{2,0},{3,1},{4,6},{5,7},{6,4},{7,5},{8,10},{9,11},{10,... | collective-permute-start | bytes 294920 | tf_op jit(solution)/shard_map/ppermute | solution.py:57
  36.9 2.3 %collective-permute-done.9 = f32[192,128]{1,0:T(8,128)S(1)} collective-permute-done((f32[192,128]{1,0:T(8,128)S(1)}, f32[192,128]{1,0:T(8,128)S(1)}, u32[]{:S(2)}, u32[]{:S(2)}) %collective-permute-start.9) | collective-permute-done | bytes 98336 | tf_op jit(solution)/shard_map/ppermute | solution.py:57
  39.2 3.7 %collective-permute-start.10 = (f32[192,128]{1,0:T(8,128)S(1)}, f32[192,128]{1,0:T(8,128)S(1)}, u32[]{:S(2)}, u32[]{:S(2)}) collective-permute-start(f32[192,128]{1,0:T(8,128)S(1)} %add.99), channel_id=1, source_target_pairs={{0,6},{1,7},{2,4},{3,5},{4,2},{5,3},{6,0},{7,1},{8,14},{9,15},{10,... | collective-permute-start | bytes 294920 | tf_op jit(solution)/shard_map/ppermute | solution.py:57
  42.9 2.3 %collective-permute-done.10 = f32[192,128]{1,0:T(8,128)S(1)} collective-permute-done((f32[192,128]{1,0:T(8,128)S(1)}, f32[192,128]{1,0:T(8,128)S(1)}, u32[]{:S(2)}, u32[]{:S(2)}) %collective-permute-start.10) | collective-permute-done | bytes 98336 | tf_op jit(solution)/shard_map/ppermute | solution.py:57
  45.2 2.5 %collective-permute-start.11 = (f32[192,128]{1,0:T(8,128)S(1)}, f32[192,128]{1,0:T(8,128)S(1)}, u32[]{:S(2)}, u32[]{:S(2)}) collective-permute-start(f32[192,128]{1,0:T(8,128)S(1)} %add.100), channel_id=1, source_target_pairs={{0,96},{1,25},{2,98},{3,27},{4,100},{5,29},{6,102},{7,31},{8,104},... | collective-permute-start | bytes 294920 | tf_op jit(solution)/shard_map/ppermute | solution.py:57
  47.7 3.7 %collective-permute-done.11 = f32[192,128]{1,0:T(8,128)S(1)} collective-permute-done((f32[192,128]{1,0:T(8,128)S(1)}, f32[192,128]{1,0:T(8,128)S(1)}, u32[]{:S(2)}, u32[]{:S(2)}) %collective-permute-start.11) | collective-permute-done | bytes 98336 | tf_op jit(solution)/shard_map/ppermute | solution.py:57
  51.4 5.7 %collective-permute-done.6 = f32[4,256,256]{2,1,0:T(8,128)S(1)} collective-permute-done((f32[4,256,256]{2,1,0:T(8,128)S(1)}, f32[4,256,256]{2,1,0:T(8,128)S(1)}, u32[]{:S(2)}, u32[]{:S(2)}) %collective-permute-start.6) | collective-permute-done | bytes 1048608 | tf_op jit(solution)/shard_map/ppermute | solution.py:44
  57.1 0.2 add_bitcast_fusion
  57.4 1.8 %collective-permute-start.13 = (f32[256,256]{1,0:T(8,128)S(1)}, f32[256,256]{1,0:T(8,128)S(1)}, u32[]{:S(2)}, u32[]{:S(2)}) collective-permute-start(f32[256,256]{1,0:T(8,128)S(1)} %get-tuple-element.70), channel_id=1, source_target_pairs={{0,64},{1,17},{2,66},{3,19},{4,68},{5,21},{6,70},{7,23},{8,72},{9,... | collective-permute-start | bytes 786440 | tf_op jit(solution)/shard_map/ppermute | solution.py:44
  59.1 0.8 collective-permute-start.14
  60.0 1.8 %collective-permute-start.15 = (f32[256,256]{1,0:T(8,128)S(1)}, f32[256,256]{1,0:T(8,128)S(1)}, u32[]{:S(2)}, u32[]{:S(2)}) collective-permute-start(f32[256,256]{1,0:T(8,128)S(1)} %get-tuple-element.68), channel_id=1, source_target_pairs={{0,96},{1,25},{2,98},{3,27},{4,100},{5,29},{6,102},{7,31},{8,104},... | collective-permute-start | bytes 786440 | tf_op jit(solution)/shard_map/ppermute | solution.py:44
  61.8 2.2 %collective-permute-start.12 = (f32[192,128]{1,0:T(8,128)S(1)}, f32[192,128]{1,0:T(8,128)S(1)}, u32[]{:S(2)}, u32[]{:S(2)}) collective-permute-start(f32[192,128]{1,0:T(8,128)S(1)} %add.101.mine), channel_id=1, source_target_pairs={{0,1},{1,0},{2,3},{3,2},{4,5},{5,4},{6,7},{7,6},{8,9},{9,8},{10,11... | collective-permute-start | bytes 294920 | tf_op jit(solution)/shard_map/ppermute | solution.py:48
  64.0 0.5 collective-permute-done.13
  64.5 2.8 %collective-permute-done.14 = f32[256,256]{1,0:T(8,128)S(1)} collective-permute-done((f32[256,256]{1,0:T(8,128)S(1)}, f32[256,256]{1,0:T(8,128)S(1)}, u32[]{:S(2)}, u32[]{:S(2)}) %collective-permute-start.14) | collective-permute-done | bytes 262176 | tf_op jit(solution)/shard_map/ppermute | solution.py:44
  67.3 0.0 collective-permute-done.15
  67.3 0.1 fusion
  67.4 0.0 collective-permute-done.12.other
  67.4 3.7 %collective-permute-start.16 = (f32[256,256]{1,0:T(8,128)S(1)}, f32[256,256]{1,0:T(8,128)S(1)}, u32[]{:S(2)}, u32[]{:S(2)}) collective-permute-start(f32[256,256]{1,0:T(8,128)S(1)} %fusion), channel_id=1, source_target_pairs={{0,4},{1,5},{2,6},{3,7},{4,0},{5,1},{6,2},{7,3},{8,12},{9,13},{10,... | collective-permute-start | bytes 786440 | tf_op jit(solution)/shard_map/ppermute | solution.py:44
  71.1 0.5 collective-permute-start.17
  71.6 1.0 %collective-permute-start.18 = (f32[256,256]{1,0:T(8,128)S(1)}, f32[256,256]{1,0:T(8,128)S(1)}, u32[]{:S(2)}, u32[]{:S(2)}) collective-permute-start(f32[256,256]{1,0:T(8,128)S(1)} %fusion), channel_id=1, source_target_pairs={{0,2},{1,3},{2,4},{3,5},{4,6},{5,7},{6,0},{7,1},{8,10},{9,11},{10,... | collective-permute-start | bytes 786440 | tf_op jit(solution)/shard_map/ppermute | solution.py:44
  72.6 8.5 %inverse.1.refs_1_ = f32[256,256]{1,0:T(8,128)S(1)} custom-call(s32[5]{0:T(128)S(1)} %stack.23.place.refs_0_.refs_3_, f32[192,128]{1,0:T(8,128)S(1)} %add.101.mine, f32[192,128]{1,0:T(8,128)S(1)} %collective-permute-done.12.other), custom_call_target="tpu_custom_call" | custom-call | flops 8000000000 | bytes 4194304 | tf_op jit(solution)/shard_map/inverse/pallas_call | solution.py:266
  81.1 2.0 %convolution_multiply_fusion = f32[1024,256]{1,0:T(8,128)} fusion(f32[1024,256]{1,0:T(8,128)S(1)} %get-tuple-element.59, f32[256,256]{1,0:T(8,128)S(1)} %inverse.1.refs_1_), kind=kOutput, calls=%fused_computation | convolution fusion | flops 805568512 | bytes 2359296 | tf_op jit(solution)/shard_map/dot_general | solution.py:331
  83.1 0.0 collective-permute-done.16
  83.1 0.1 collective-permute-done.17
  83.2 0.1 add_add_fusion.refs_2_
  83.3 2.0 %collective-permute-start.19 = (f32[256,256]{1,0:T(8,128)S(1)}, f32[256,256]{1,0:T(8,128)S(1)}, u32[]{:S(2)}, u32[]{:S(2)}) collective-permute-start(f32[256,256]{1,0:T(8,128)S(1)} %add_add_fusion.refs_2_), channel_id=1, source_target_pairs={{0,1},{1,0},{2,3},{3,2},{4,5},{5,4},{6,7},{7,6},{8,9},{9,8},{10,11... | collective-permute-start | bytes 786440 | tf_op jit(solution)/shard_map/ppermute | solution.py:48
  85.3 1.0 %finish_mine.1.refs_3_ = f32[256,256]{1,0:T(8,128)S(1)} custom-call(s32[5]{0:T(128)S(1)} %stack.23.place.refs_0_.refs_3_, f32[256,256]{1,0:T(8,128)S(1)} %inverse.1.refs_1_, f32[256,256]{1,0:T(8,128)S(1)} %add_add_fusion.refs_2_), custom_call_target="tpu_custom_call" | custom-call | flops 1000000000 | bytes 4194304 | tf_op jit(solution)/shard_map/finish_mine/pallas_call | solution.py:266
  86.3 0.2 collective-permute-done.19.refs_2_
  86.5 1.8 %finish.1 = f32[512,256]{1,0:T(8,128)} custom-call(s32[5]{0:T(128)S(1)} %stack.23.place.refs_0_.refs_3_, f32[256,256]{1,0:T(8,128)S(1)} %inverse.1.refs_1_, f32[256,256]{1,0:T(8,128)S(1)} %collective-permute-done.19.refs_2_, f32[256,256]{1,0:T(8,128)S(1)} %finish_mine.1.refs_3_), custom_call_target="tpu_custom_call" | custom-call | flops 1000000000 | bytes 4194304 | tf_op jit(solution)/shard_map/finish/pallas_call | solution.py:266
  (12 shorter events, 0.1 us)
Async XLA Ops:
  11.4 4.5 %collective-permute-start = (f32[192,128]{1,0:T(8,128)S(1)}, f32[192,128]{1,0:T(8,128)S(1)}, u32[]{:S(2)}, u32[]{:S(2)}) collective-permute-start(f32[192,128]{1,0:T(8,128)S(1)} %get-tuple-element.36), channel_id=1, source_target_pairs={{0,1},{1,0},{2,3},{3,2},{4,5},{5,4},{6,7},{7,6},{8,9},{9,8},{10,11... | collective-permute-start | bytes 294920 | tf_op jit(solution)/shard_map/ppermute | solution.py:48
  15.8 8.4 %collective-permute-start.3 = (f32[8,256,256]{2,1,0:T(8,128)S(1)}, f32[8,256,256]{2,1,0:T(8,128)S(1)}, u32[]{:S(2)}, u32[]{:S(2)}) collective-permute-start(f32[8,256,256]{2,1,0:T(8,128)S(1)} %projection.5), channel_id=1, source_target_pairs={{0,1},{1,0},{2,3},{3,2},{4,5},{5,4},{6,7},{7,6},{8,9},{9,8},{10,11... | collective-permute-start | bytes 6291464 | tf_op jit(solution)/shard_map/ppermute | solution.py:48
  15.9 4.3 %collective-permute-start.1 = (f32[192,128]{1,0:T(8,128)S(1)}, f32[192,128]{1,0:T(8,128)S(1)}, u32[]{:S(2)}, u32[]{:S(2)}) collective-permute-start(f32[192,128]{1,0:T(8,128)S(1)} %add.95.refs_3_), channel_id=1, source_target_pairs={{0,8},{1,33},{2,10},{3,35},{4,12},{5,37},{6,14},{7,39},{8,0},{9,41... | collective-permute-start | bytes 294920 | tf_op jit(solution)/shard_map/ppermute | solution.py:57
  20.3 9.1 %collective-permute-start.5 = (f32[8,256,256]{2,1,0:T(8,128)S(1)}, f32[8,256,256]{2,1,0:T(8,128)S(1)}, u32[]{:S(2)}, u32[]{:S(2)}) collective-permute-start(f32[8,256,256]{2,1,0:T(8,128)S(1)} %projection.4), channel_id=1, source_target_pairs={{0,1},{1,0},{2,3},{3,2},{4,5},{5,4},{6,7},{7,6},{8,9},{9,8},{10,11... | collective-permute-start | bytes 6291464 | tf_op jit(solution)/shard_map/ppermute | solution.py:48
  21.1 6.0 %collective-permute-start.2 = (f32[192,128]{1,0:T(8,128)S(1)}, f32[192,128]{1,0:T(8,128)S(1)}, u32[]{:S(2)}, u32[]{:S(2)}) collective-permute-start(f32[192,128]{1,0:T(8,128)S(1)} %add.96.refs_3_), channel_id=1, source_target_pairs={{0,24},{1,97},{2,26},{3,99},{4,28},{5,101},{6,30},{7,103},{8,16},{... | collective-permute-start | bytes 294920 | tf_op jit(solution)/shard_map/ppermute | solution.py:57
  27.1 5.2 %collective-permute-start.4 = (f32[192,128]{1,0:T(8,128)S(1)}, f32[192,128]{1,0:T(8,128)S(1)}, u32[]{:S(2)}, u32[]{:S(2)}) collective-permute-start(f32[192,128]{1,0:T(8,128)S(1)} %add.97.refs_3_), channel_id=1, source_target_pairs={{0,32},{1,9},{2,34},{3,11},{4,36},{5,13},{6,38},{7,15},{8,40},{9,1... | collective-permute-start | bytes 294920 | tf_op jit(solution)/shard_map/ppermute | solution.py:57
  28.4 22.9 %collective-permute-start.7 = (f32[4,256,256]{2,1,0:T(8,128)S(1)}, f32[4,256,256]{2,1,0:T(8,128)S(1)}, u32[]{:S(2)}, u32[]{:S(2)}) collective-permute-start(f32[4,256,256]{2,1,0:T(8,128)S(1)} %get-tuple-element.50), channel_id=1, source_target_pairs={{0,16},{1,65},{2,18},{3,67},{4,20},{5,69},{6,22},{7,71},{8,24},{9,... | collective-permute-start | bytes 3145736 | tf_op jit(solution)/shard_map/ppermute | solution.py:44
  32.4 24.7 %collective-permute-start.6 = (f32[4,256,256]{2,1,0:T(8,128)S(1)}, f32[4,256,256]{2,1,0:T(8,128)S(1)}, u32[]{:S(2)}, u32[]{:S(2)}) collective-permute-start(f32[4,256,256]{2,1,0:T(8,128)S(1)} %get-tuple-element.49), channel_id=1, source_target_pairs={{0,8},{1,33},{2,10},{3,35},{4,12},{5,37},{6,14},{7,39},{8,16},{9,4... | collective-permute-start | bytes 3145736 | tf_op jit(solution)/shard_map/ppermute | solution.py:44
  33.8 23.4 %collective-permute-start.8 = (f32[4,256,256]{2,1,0:T(8,128)S(1)}, f32[4,256,256]{2,1,0:T(8,128)S(1)}, u32[]{:S(2)}, u32[]{:S(2)}) collective-permute-start(f32[4,256,256]{2,1,0:T(8,128)S(1)} %get-tuple-element.51), channel_id=1, source_target_pairs={{0,24},{1,97},{2,26},{3,99},{4,28},{5,101},{6,30},{7,103},{8,0},{9... | collective-permute-start | bytes 3145736 | tf_op jit(solution)/shard_map/ppermute | solution.py:44
  35.1 4.0 %collective-permute-start.9 = (f32[192,128]{1,0:T(8,128)S(1)}, f32[192,128]{1,0:T(8,128)S(1)}, u32[]{:S(2)}, u32[]{:S(2)}) collective-permute-start(f32[192,128]{1,0:T(8,128)S(1)} %add.98), channel_id=1, source_target_pairs={{0,2},{1,3},{2,0},{3,1},{4,6},{5,7},{6,4},{7,5},{8,10},{9,11},{10,... | collective-permute-start | bytes 294920 | tf_op jit(solution)/shard_map/ppermute | solution.py:57
  39.2 6.0 %collective-permute-start.10 = (f32[192,128]{1,0:T(8,128)S(1)}, f32[192,128]{1,0:T(8,128)S(1)}, u32[]{:S(2)}, u32[]{:S(2)}) collective-permute-start(f32[192,128]{1,0:T(8,128)S(1)} %add.99), channel_id=1, source_target_pairs={{0,6},{1,7},{2,4},{3,5},{4,2},{5,3},{6,0},{7,1},{8,14},{9,15},{10,... | collective-permute-start | bytes 294920 | tf_op jit(solution)/shard_map/ppermute | solution.py:57
  45.2 6.2 %collective-permute-start.11 = (f32[192,128]{1,0:T(8,128)S(1)}, f32[192,128]{1,0:T(8,128)S(1)}, u32[]{:S(2)}, u32[]{:S(2)}) collective-permute-start(f32[192,128]{1,0:T(8,128)S(1)} %add.100), channel_id=1, source_target_pairs={{0,96},{1,25},{2,98},{3,27},{4,100},{5,29},{6,102},{7,31},{8,104},... | collective-permute-start | bytes 294920 | tf_op jit(solution)/shard_map/ppermute | solution.py:57
  57.4 7.1 %collective-permute-start.13 = (f32[256,256]{1,0:T(8,128)S(1)}, f32[256,256]{1,0:T(8,128)S(1)}, u32[]{:S(2)}, u32[]{:S(2)}) collective-permute-start(f32[256,256]{1,0:T(8,128)S(1)} %get-tuple-element.70), channel_id=1, source_target_pairs={{0,64},{1,17},{2,66},{3,19},{4,68},{5,21},{6,70},{7,23},{8,72},{9,... | collective-permute-start | bytes 786440 | tf_op jit(solution)/shard_map/ppermute | solution.py:44
  59.1 8.1 %collective-permute-start.14 = (f32[256,256]{1,0:T(8,128)S(1)}, f32[256,256]{1,0:T(8,128)S(1)}, u32[]{:S(2)}, u32[]{:S(2)}) collective-permute-start(f32[256,256]{1,0:T(8,128)S(1)} %get-tuple-element.69), channel_id=1, source_target_pairs={{0,32},{1,9},{2,34},{3,11},{4,36},{5,13},{6,38},{7,15},{8,40},{9,1... | collective-permute-start | bytes 786440 | tf_op jit(solution)/shard_map/ppermute | solution.py:44
  60.0 7.3 %collective-permute-start.15 = (f32[256,256]{1,0:T(8,128)S(1)}, f32[256,256]{1,0:T(8,128)S(1)}, u32[]{:S(2)}, u32[]{:S(2)}) collective-permute-start(f32[256,256]{1,0:T(8,128)S(1)} %get-tuple-element.68), channel_id=1, source_target_pairs={{0,96},{1,25},{2,98},{3,27},{4,100},{5,29},{6,102},{7,31},{8,104},... | collective-permute-start | bytes 786440 | tf_op jit(solution)/shard_map/ppermute | solution.py:44
  61.8 5.6 %collective-permute-start.12 = (f32[192,128]{1,0:T(8,128)S(1)}, f32[192,128]{1,0:T(8,128)S(1)}, u32[]{:S(2)}, u32[]{:S(2)}) collective-permute-start(f32[192,128]{1,0:T(8,128)S(1)} %add.101.mine), channel_id=1, source_target_pairs={{0,1},{1,0},{2,3},{3,2},{4,5},{5,4},{6,7},{7,6},{8,9},{9,8},{10,11... | collective-permute-start | bytes 294920 | tf_op jit(solution)/shard_map/ppermute | solution.py:48
  67.4 15.6 %collective-permute-start.16 = (f32[256,256]{1,0:T(8,128)S(1)}, f32[256,256]{1,0:T(8,128)S(1)}, u32[]{:S(2)}, u32[]{:S(2)}) collective-permute-start(f32[256,256]{1,0:T(8,128)S(1)} %fusion), channel_id=1, source_target_pairs={{0,4},{1,5},{2,6},{3,7},{4,0},{5,1},{6,2},{7,3},{8,12},{9,13},{10,... | collective-permute-start | bytes 786440 | tf_op jit(solution)/shard_map/ppermute | solution.py:44
  71.1 12.1 %collective-permute-start.17 = (f32[256,256]{1,0:T(8,128)S(1)}, f32[256,256]{1,0:T(8,128)S(1)}, u32[]{:S(2)}, u32[]{:S(2)}) collective-permute-start(f32[256,256]{1,0:T(8,128)S(1)} %fusion), channel_id=1, source_target_pairs={{0,6},{1,7},{2,0},{3,1},{4,2},{5,3},{6,4},{7,5},{8,14},{9,15},{10,... | collective-permute-start | bytes 786440 | tf_op jit(solution)/shard_map/ppermute | solution.py:44
  71.6 11.6 %collective-permute-start.18 = (f32[256,256]{1,0:T(8,128)S(1)}, f32[256,256]{1,0:T(8,128)S(1)}, u32[]{:S(2)}, u32[]{:S(2)}) collective-permute-start(f32[256,256]{1,0:T(8,128)S(1)} %fusion), channel_id=1, source_target_pairs={{0,2},{1,3},{2,4},{3,5},{4,6},{5,7},{6,0},{7,1},{8,10},{9,11},{10,... | collective-permute-start | bytes 786440 | tf_op jit(solution)/shard_map/ppermute | solution.py:44
  83.3 3.2 %collective-permute-start.19 = (f32[256,256]{1,0:T(8,128)S(1)}, f32[256,256]{1,0:T(8,128)S(1)}, u32[]{:S(2)}, u32[]{:S(2)}) collective-permute-start(f32[256,256]{1,0:T(8,128)S(1)} %add_add_fusion.refs_2_), channel_id=1, source_target_pairs={{0,1},{1,0},{2,3},{3,2},{4,5},{5,4},{6,7},{7,6},{8,9},{9,8},{10,11... | collective-permute-start | bytes 786440 | tf_op jit(solution)/shard_map/ppermute | solution.py:48
